TPU v7x, 1024 devices: a whole 4x4x32 slice. The times are simulated.
1024 devices in a mesh: dp: 128 (over x_lo, z, core), mp: 8 (over y, x_hi).
Axes of the slice: x: 4 (x_hi: 2, x_lo: 2; x = x_hi * 2 + x_lo), y: 4, z: 32, core: 2. Of those that a mesh axis runs over, the one named last changes fastest.
Arguments:
- queries: bfloat16 [65536, 3072], P('dp', 'mp'), may hold values from -25 to 25
- keys: bfloat16 [65536, 3072], P('dp', 'mp'), may hold values from -8 to 8
- values: bfloat16 [65536, 3072], P('dp', 'mp'), may hold values from -6 to 6
- grad_out: bfloat16 [65536, 3072], P('dp', 'mp'), may hold values from -0.375 to 0.375
- out_weight: bfloat16 [3072, 3072], P('dp', 'mp'), may hold values from -1.75 to 1.75
Outputs:
- d_queries: bfloat16 [65536, 3072], P('dp', 'mp')
- d_keys: bfloat16 [65536, 3072], P('dp', 'mp')
- d_values: bfloat16 [65536, 3072], P('dp', 'mp')
All inputs are finite; a program needn't handle non-finite values.
Results may differ from a plain program's by a relative error of at most 0.0075.
Values may be sent and summed in bfloat16 or wider, within the bound.
No kernel may reach another device: no remote copies, remote signals or barrier semaphores. Data moves between devices by JAX's collectives and lax.ppermute only.
A program may use at most 32 MiB of HBM per device.

v0:
```python
import math

import jax
import jax.numpy as jnp
from jax import lax
from jax.sharding import PartitionSpec as P

HEAD_SIZE = 128
PATCHES = 256


def body(queries, keys, values, grad_out, out_weight):
    tok_rows = queries.shape[0]
    images = tok_rows // PATCHES
    heads_here = queries.shape[1] // HEAD_SIZE
    width_here = queries.shape[1]
    score_scale = 1.0 / math.sqrt(HEAD_SIZE)

    def split_heads(array):
        return array.reshape(images, PATCHES, heads_here, HEAD_SIZE)

    whole_grad = lax.all_gather(grad_out, "mp", axis=1, tiled=True)
    full_weight = lax.all_gather(out_weight, "dp", axis=0, tiled=True)
    grad_total = jnp.dot(whole_grad, full_weight, preferred_element_type=jnp.float32)
    query_img = split_heads(queries)
    key_img = split_heads(keys)
    value_img = split_heads(values)
    scores = (
        jnp.einsum("iqhd,ikhd->ihqk", query_img, key_img, preferred_element_type=jnp.float32)
        * score_scale
    )
    probs = jax.nn.softmax(scores, axis=-1)
    probs_half = probs.astype(jnp.bfloat16)
    grad_img = split_heads(grad_total.astype(jnp.bfloat16))
    d_values = jnp.einsum(
        "ihqk,iqhd->ikhd", probs_half, grad_img, preferred_element_type=jnp.float32
    ).astype(jnp.bfloat16)
    d_probs = jnp.einsum("iqhd,ikhd->ihqk", grad_img, value_img, preferred_element_type=jnp.float32)
    row_dot = jnp.sum(probs * d_probs, axis=-1, keepdims=True)
    d_scores = (probs * (d_probs - row_dot)).astype(jnp.bfloat16)
    d_queries = (
        jnp.einsum("ihqk,ikhd->iqhd", d_scores, key_img, preferred_element_type=jnp.float32)
        * score_scale
    ).astype(jnp.bfloat16)
    d_keys = (
        jnp.einsum("ihqk,iqhd->ikhd", d_scores, query_img, preferred_element_type=jnp.float32)
        * score_scale
    ).astype(jnp.bfloat16)
    return (
        d_queries.reshape(tok_rows, width_here),
        d_keys.reshape(tok_rows, width_here),
        d_values.reshape(tok_rows, width_here),
    )


def solution(mesh):
    placed = (P("dp", "mp"), P("dp", "mp"), P("dp", "mp"), P("dp", "mp"), P("dp", "mp"))
    return jax.shard_map(
        body,
        mesh=mesh,
        in_specs=placed,
        out_specs=(P("dp", "mp"), P("dp", "mp"), P("dp", "mp")),
        check_vma=False,
    )
```

profile of v0, /device:TPU:1, one launch (start us, length us, event | category | flops | bytes accessed | tf_op | source)
XLA Modules:
  0.0 370.4 jit_solution(6515928091826789833)
XLA Ops:
  7.2 0.0 copy-start.1
  7.2 0.0 copy-start.2
  7.2 0.0 all-gather.5.cloned.1.call-start
  7.2 0.7 all-gather.5.cloned.1.call-update
  7.9 0.0 all-gather.3.cloned.1.call-start
  8.0 0.7 all-gather.3.cloned.1.call-update
  8.7 1.4 reshape.41
  10.1 0.0 copy-done.1
  10.1 0.1 reshape.42
  10.2 0.0 copy-done.2
  10.2 0.9 reshape.37
  11.1 0.7 fusion.25
  11.8 244.0 %all-gather.5.cloned.1.call-done = bf16[3072,384]{1,0:T(8,128)(2,1)} async-done(((bf16[24,384]{1,0:T(8,128)(2,1)}), bf16[3072,384]{1,0:T(8,128)(2,1)}) %all-gather.5.cloned.1.call-update) | async-done | bytes 2359312 | tf_op jit(solution)/shard_map/all_gather | solution.py:23
  255.7 96.4 %all-gather.3.cloned.1.call-done = bf16[512,3072]{1,0:T(8,128)(2,1)} async-done(((bf16[512,384]{1,0:T(8,128)(2,1)}), bf16[512,3072]{1,0:T(8,128)(2,1)}) %all-gather.3.cloned.1.call-update) | async-done | bytes 3145744 | tf_op jit(solution)/shard_map/all_gather | solution.py:22
  352.2 4.4 %convolution_convert_fusion.1 = bf16[512,384]{1,0:T(8,128)(2,1)S(1)} fusion(bf16[512,3072]{1,0:T(8,128)(2,1)} %all-gather.3.cloned.1.call-done, bf16[3072,384]{1,0:T(8,128)(2,1)} %all-gather.5.cloned.1.call-done), kind=kOutput, calls=%fused_computation.11 | convolution fusion | flops 1208156160 | bytes 5898240 | tf_op jit(solution)/shard_map/dot_general | solution.py:24
  356.6 0.1 reshape.43
  356.7 1.0 copy.30
  357.7 0.0 copy-start
  357.7 0.0 copy-start.3
  357.7 1.5 fusion.7
  359.2 0.0 copy-done
  359.2 0.0 copy-done.3
  359.2 0.4 multiply_reduce_fusion
  359.6 0.4 multiply_convert_fusion
  359.9 0.4 fusion.5
  360.3 0.4 fusion.6
  360.7 0.3 copy.42
  361.0 0.3 copy.40
  361.4 0.8 copy.82
  362.2 0.3 copy.41
  362.5 1.0 copy_bitcast_fusion
Async XLA Ops:
  7.2 2.9 copy-start.1
  7.2 3.0 copy-start.2
  7.2 248.6 %all-gather.5.cloned.1.call-start = ((), (), s32[]{:S(2)}) async-start(), calls=%async_computation.1 | async-start | bytes 2377728 | tf_op jit(solution)/shard_map/all_gather | solution.py:23
  7.9 344.3 %all-gather.3.cloned.1.call-start = ((), (), s32[]{:S(2)}) async-start(), calls=%async_computation | async-start | bytes 3538944 | tf_op jit(solution)/shard_map/all_gather | solution.py:22
  357.7 1.5 copy-start
  357.7 1.5 copy-start.3
Sparse Core Ops, SparseCore 0:
  10.8 244.9 all-gather.4
  260.0 92.1 all-gather.2
where the time goes:
time: 371 us; the launch traced here: 370 us
  waiting for transfers between devices  342 us (92%)
  between operations  14.2 us (4%)
  matrix products  7.69 us (2%)
  local copies, waits for them, and re-layouts  6.3 us (2%)
    all_gather x1, waiting for transfers between devices, body(): full_weight = lax.all_gather(out_weight, 'dp', axis=0, tiled=True)  244 us
    all_gather x1, waiting for transfers between devices, body(): whole_grad = lax.all_gather(grad_out, 'mp', axis=1, tiled=True)  96.4 us
  transfers between devices with their start and end apart: 2, of which 2 were waited for; matrix products, arithmetic and copies ran while one was open for 1% of the time, Pallas kernels for 0%

commit v1 on v0

--- a/solution.py
+++ b/solution.py
@@ -7,6 +7,67 @@
 
 HEAD_SIZE = 128
 PATCHES = 256
+XLO, Z, CORES = 2, 32, 2
+STRIDE = 4
+FAR = Z // STRIDE
+
+
+def dp_index(x, z, c):
+    return (x * Z + z % Z) * CORES + c
+
+
+def everyone():
+    return [(x, z, c) for x in range(XLO) for z in range(Z) for c in range(CORES)]
+
+
+def far_groups():
+    return [
+        [dp_index(x, r + STRIDE * k, c) for k in range(FAR)]
+        for x in range(XLO)
+        for r in range(STRIDE)
+        for c in range(CORES)
+    ]
+
+
+def z_shift(array, step):
+    pairs = [
+        (dp_index(x, z + (step if c == 0 else -step), c), dp_index(x, z, c))
+        for x, z, c in everyone()
+    ]
+    return lax.ppermute(array, "dp", pairs)
+
+
+def gather_weight(weight):
+    rows, width = weight.shape
+    here = lax.axis_index("dp")
+    core = here % CORES
+    z = (here // CORES) % Z
+    x = here // (CORES * Z)
+    far = lax.all_to_all(
+        jnp.broadcast_to(weight[None], (FAR, rows, width)),
+        "dp",
+        0,
+        0,
+        tiled=True,
+        axis_index_groups=far_groups(),
+    )
+    sign = 1 - 2 * core
+    residue = z % STRIDE
+    parts = [(far, residue)]
+    for step in (1, -1, 2):
+        parts.append((z_shift(far, step), (residue + sign * step) % STRIDE))
+    column = jnp.zeros((FAR, STRIDE, rows, width), weight.dtype)
+    for part, where in parts:
+        column = lax.dynamic_update_slice(column, part[:, None], (0, where, 0, 0))
+    swap_x = [(dp_index(a, b, c), dp_index(1 - a, b, c)) for a, b, c in everyone()]
+    other = lax.ppermute(column, "dp", swap_x)
+    both = jnp.where(x == 0, jnp.stack([column, other]), jnp.stack([other, column]))
+    swap_c = [(dp_index(a, b, c), dp_index(a, b, 1 - c)) for a, b, c in everyone()]
+    across = lax.ppermute(both, "dp", swap_c)
+    whole = jnp.where(
+        core == 0, jnp.stack([both, across], axis=3), jnp.stack([across, both], axis=3)
+    )
+    return whole.reshape(XLO * Z * CORES * rows, width)
 
 
 def body(queries, keys, values, grad_out, out_weight):
@@ -19,9 +80,17 @@
     def split_heads(array):
         return array.reshape(images, PATCHES, heads_here, HEAD_SIZE)
 
-    whole_grad = lax.all_gather(grad_out, "mp", axis=1, tiled=True)
-    full_weight = lax.all_gather(out_weight, "dp", axis=0, tiled=True)
-    grad_total = jnp.dot(whole_grad, full_weight, preferred_element_type=jnp.float32)
+    pieces = 8
+    blocks = lax.all_to_all(
+        jnp.broadcast_to(grad_out[None], (pieces, tok_rows, width_here)), "mp", 0, 0, tiled=True
+    )
+    full_weight = gather_weight(out_weight)
+    grad_total = jnp.einsum(
+        "jtk,jkn->tn",
+        blocks,
+        full_weight.reshape(pieces, width_here, width_here),
+        preferred_element_type=jnp.float32,
+    )
     query_img = split_heads(queries)
     key_img = split_heads(keys)
     value_img = split_heads(values)

time: 371 us -> 141 us (0.38)
  the two profiles are of different devices: /device:TPU:1 before, /device:TPU:69 now
where the time goes in v1:
time: 141 us
  waiting for transfers between devices  67.5 us (48%)
  starting transfers between devices  48.3 us (34%)
  local copies, waits for them, and re-layouts  11.9 us (8%)
  matrix products  8.97 us (6%)
  other arithmetic  2.97 us (2%)
    ppermute x1, waiting for transfers between devices, gather_weight(): other = lax.ppermute(column, 'dp', swap_x)  31.6 us
    all_to_all x1, waiting for transfers between devices, gather_weight(): lax.all_to_all(jnp.broadcast_to(weight[None], (FAR, rows, width)), 'dp',...  31.1 us
    all_to_all x1, starting transfers between devices, gather_weight(): lax.all_to_all(jnp.broadcast_to(weight[None], (FAR, rows, width)), 'dp',...  26.3 us
    ppermute x3, starting transfers between devices, z_shift(): return lax.ppermute(array, 'dp', pairs)  8.52 us
    all_to_all x1, starting transfers between devices, body(): lax.all_to_all(jnp.broadcast_to(grad_out[None], (pieces, tok_rows, width_...  6.87 us
    ppermute x3, waiting for transfers between devices, z_shift(): return lax.ppermute(array, 'dp', pairs)  4.9 us
    reshape x4, local copies, waits for them, and re-layouts, split_heads(): return array.reshape(images, PATCHES, heads_here, HEAD_SIZE)  4.67 us
    dot_general x1, matrix products, body(): jnp.einsum('jtk,jkn->tn', blocks, full_weight.reshape(pieces, width_here,...  4.07 us
  transfers between devices with their start and end apart: 7, of which 4 were waited for; matrix products, arithmetic and copies ran while one was open for 6% of the time, Pallas kernels for 0%

profile of v1, /device:TPU:69, one launch (start us, length us, event | category | flops | bytes accessed | tf_op | source)
XLA Modules:
  0.0 140.6 jit_solution(8005242409851427985)
XLA Ops:
  0.6 1.4 broadcast_in_dim.15
  2.0 26.3 %all-to-all-start = ((bf16[8,24,384]{2,1,0:T(8,128)(2,1)}), bf16[8,24,384]{2,1,0:T(8,128)(2,1)S(1)}, u32[]{:S(2)}, u32[]{:S(2)}) async-start(bf16[8,24,384]{2,1,0:T(8,128)(2,1)} %broadcast_in_dim.15), calls=%async_computation | async-start | bytes 294912 | tf_op jit(solution)/shard_map/all_to_all | solution.py:46
  28.3 31.1 %all-to-all-done = bf16[8,24,384]{2,1,0:T(8,128)(2,1)S(1)} async-done(((bf16[8,24,384]{2,1,0:T(8,128)(2,1)}), bf16[8,24,384]{2,1,0:T(8,128)(2,1)S(1)}, u32[]{:S(2)}, u32[]{:S(2)}) %all-to-all-start) | async-done | bytes 147488 | tf_op jit(solution)/shard_map/all_to_all | solution.py:46
  59.3 3.0 %broadcast_in_dim.36 = bf16[8,512,384]{2,1,0:T(8,128)(2,1)} broadcast(bf16[512,384]{1,0:T(8,128)(2,1)} %param.8), dimensions={1,2} | broadcast | bytes 3538944 | tf_op jit(solution)/shard_map/broadcast_in_dim | solution.py:85
  62.3 6.9 %all-to-all-start.1 = ((bf16[8,512,384]{2,1,0:T(8,128)(2,1)}), bf16[8,512,384]{2,1,0:T(8,128)(2,1)}, u32[]{:S(2)}, u32[]{:S(2)}) async-start(bf16[8,512,384]{2,1,0:T(8,128)(2,1)} %broadcast_in_dim.36), calls=%async_computation.1 | async-start | bytes 6291456 | tf_op jit(solution)/shard_map/all_to_all | solution.py:84
  69.2 1.9 %collective-permute-start = (bf16[8,24,384]{2,1,0:T(8,128)(2,1)S(1)}, bf16[8,24,384]{2,1,0:T(8,128)(2,1)S(1)}, u32[]{:S(2)}, u32[]{:S(2)}) collective-permute-start(bf16[8,24,384]{2,1,0:T(8,128)(2,1)S(1)} %all-to-all-done), channel_id=1, source_target_pairs={{16,0},{504,8},{32,16},{8,24},{48,32},{24,40},{64,48},{40,56},{80,... | collective-permute-start | bytes 442376 | tf_op jit(solution)/shard_map/ppermute | solution.py:37
  71.1 3.4 %collective-permute-start.1 = (bf16[8,24,384]{2,1,0:T(8,128)(2,1)S(1)}, bf16[8,24,384]{2,1,0:T(8,128)(2,1)S(1)}, u32[]{:S(2)}, u32[]{:S(2)}) collective-permute-start(bf16[8,24,384]{2,1,0:T(8,128)(2,1)S(1)} %all-to-all-done), channel_id=1, source_target_pairs={{496,0},{24,8},{0,16},{40,24},{16,32},{56,40},{32,48},{72,56},{48,... | collective-permute-start | bytes 442376 | tf_op jit(solution)/shard_map/ppermute | solution.py:37
  74.5 3.2 %collective-permute-start.2 = (bf16[8,24,384]{2,1,0:T(8,128)(2,1)S(1)}, bf16[8,24,384]{2,1,0:T(8,128)(2,1)S(1)}, u32[]{:S(2)}, u32[]{:S(2)}) collective-permute-start(bf16[8,24,384]{2,1,0:T(8,128)(2,1)S(1)} %all-to-all-done), channel_id=1, source_target_pairs={{32,0},{488,8},{48,16},{504,24},{64,32},{8,40},{80,48},{24,56},{96... | collective-permute-start | bytes 442376 | tf_op jit(solution)/shard_map/ppermute | solution.py:37
  77.9 0.9 collective-permute-done.1
  78.8 4.0 %collective-permute-done.2 = bf16[8,24,384]{2,1,0:T(8,128)(2,1)S(1)} collective-permute-done((bf16[8,24,384]{2,1,0:T(8,128)(2,1)S(1)}, bf16[8,24,384]{2,1,0:T(8,128)(2,1)S(1)}, u32[]{:S(2)}, u32[]{:S(2)}) %collective-permute-start.2) | collective-permute-done | bytes 147488 | tf_op jit(solution)/shard_map/ppermute | solution.py:37
  82.8 2.8 %collective-permute-start.3 = (bf16[8,4,24,384]{3,2,1,0:T(8,128)(2,1)S(1)}, bf16[8,4,24,384]{3,2,1,0:T(8,128)(2,1)S(1)}, u32[]{:S(2)}, u32[]{:S(2)}) collective-permute-start(bf16[8,4,24,384]{3,2,1,0:T(8,128)(2,1)S(1)} %bitcast_dynamic-update-slice_fusion.3), channel_id=1, source_target_pairs={{0,512},{8,520},{16,528},{24,536},{32,544},{40,552},{48,560},{56,5... | collective-permute-start | bytes 1769480 | tf_op jit(solution)/shard_map/ppermute | solution.py:63
  85.7 31.6 %collective-permute-done.3 = bf16[8,4,24,384]{3,2,1,0:T(8,128)(2,1)S(1)} collective-permute-done((bf16[8,4,24,384]{3,2,1,0:T(8,128)(2,1)S(1)}, bf16[8,4,24,384]{3,2,1,0:T(8,128)(2,1)S(1)}, u32[]{:S(2)}, u32[]{:S(2)}) %collective-permute-start.3) | collective-permute-done | bytes 589856 | tf_op jit(solution)/shard_map/ppermute | solution.py:63
  117.2 0.2 maximum_select_fusion.1
  117.5 3.8 %collective-permute-start.4 = (bf16[2,8,4,24,384]{4,3,2,1,0:T(8,128)(2,1)S(1)}, bf16[2,8,4,24,384]{4,3,2,1,0:T(8,128)(2,1)}, u32[]{:S(2)}, u32[]{:S(2)}) collective-permute-start(bf16[2,8,4,24,384]{4,3,2,1,0:T(8,128)(2,1)S(1)} %maximum_select_fusion.1), channel_id=1, source_target_pairs={{0,8},{8,0},{16,24},{24,16},{32,40},{40,32},{48,56},{56,48},{64,72... | collective-permute-start | bytes 3538952 | tf_op jit(solution)/shard_map/ppermute | solution.py:66
  121.3 0.1 reshape.107
  121.4 1.4 reshape.108
  122.8 2.1 %reshape.103 = bf16[2,256,3,128]{3,2,1,0:T(4,128)(2,1)} reshape(bf16[512,384]{1,0:T(8,128)(2,1)} %param.7) | data formatting | bytes 786432 | tf_op jit(solution)/shard_map/reshape | solution.py:81
  124.9 1.8 %fusion.30 = (f32[2,3,256]{2,1,0:T(4,128)S(1)}, f32[2,3,256,256]{2,3,1,0:T(8,128)}) fusion(bf16[2,256,3,128]{3,2,1,0:T(4,128)(2,1)S(1)} %reshape.108, bf16[2,256,3,128]{3,2,1,0:T(4,128)(2,1)S(1)} %reshape.107), kind=kOutput, calls=%fused_computation.41 | convolution fusion | flops 101843200 | bytes 2365440 | tf_op jit(solution)/shard_map/sub | solution.py:101
  126.7 0.2 fusion.10
  126.9 2.3 %maximum_select_fusion = bf16[2,8,4,2,24,384]{5,4,3,2,1,0:T(8,128)(2,1)S(1)} fusion(bf16[2,8,4,1,24,384]{5,4,3,2,1,0:T(8,128)(2,1)} %bitcast.13, bf16[2,8,4,1,24,384]{5,4,3,2,1,0:T(8,128)(2,1)S(1)} %fusion.10, pred[]{:T(512)S(6)} %eq.13), kind=kLoop, calls=%fused_computation.1 | loop fusion | flops 3538944 | bytes 4718593 | tf_op jit(solution)/shard_map/jit(_where)/select_n | solution.py:67
  129.2 4.1 %fusion.9 = bf16[512,384]{0,1:T(8,128)(2,1)} fusion(bf16[8,384,384]{2,1,0:T(8,128)(2,1)S(1)} %bitcast.65, bf16[8,512,384]{2,1,0:T(8,128)(2,1)} %all-to-all-done.1), kind=kOutput, calls=%fused_computation.17 | convolution fusion | flops 1208156160 | bytes 5898240 | tf_op jit(solution)/shard_map/jtk,jkn->tn/dot_general | solution.py:88
  133.3 1.1 reshape.97
  134.4 2.0 %fusion.8 = bf16[2,256,3,128]{1,3,2,0:T(8,128)(2,1)S(1)} fusion(bf16[2,256,3,128]{1,0,3,2:T(2,128)(2,1)S(1)} %reshape.97, f32[2,3,256,256]{2,3,1,0:T(8,128)} %get-tuple-element.7, f32[2,3,256]{2,1,0:T(4,128)S(1)} %get-tuple-element.6), kind=kOutput, calls=%fused_computation.16 | convolution fusion | flops 101646336 | bytes 2365440 | tf_op jit(solution)/shard_map/ihqk,iqhd->ikhd/dot_general | solution.py:104
  136.4 0.4 multiply_reduce_fusion
  136.7 0.3 multiply_convert_fusion
  137.0 0.4 fusion.6
  137.4 0.4 fusion.7
  137.8 0.3 copy.53
  138.1 0.3 copy.52
  138.5 0.3 copy.51
  138.8 0.8 copy.97
  139.6 1.0 copy_bitcast_fusion
  (14 shorter events, 0.2 us)
Async XLA Ops:
  2.0 57.3 %all-to-all-start = ((bf16[8,24,384]{2,1,0:T(8,128)(2,1)}), bf16[8,24,384]{2,1,0:T(8,128)(2,1)S(1)}, u32[]{:S(2)}, u32[]{:S(2)}) async-start(bf16[8,24,384]{2,1,0:T(8,128)(2,1)} %broadcast_in_dim.15), calls=%async_computation | async-start | bytes 294912 | tf_op jit(solution)/shard_map/all_to_all | solution.py:46
  62.3 66.9 %all-to-all-start.1 = ((bf16[8,512,384]{2,1,0:T(8,128)(2,1)}), bf16[8,512,384]{2,1,0:T(8,128)(2,1)}, u32[]{:S(2)}, u32[]{:S(2)}) async-start(bf16[8,512,384]{2,1,0:T(8,128)(2,1)} %broadcast_in_dim.36), calls=%async_computation.1 | async-start | bytes 6291456 | tf_op jit(solution)/shard_map/all_to_all | solution.py:84
  69.2 8.7 %collective-permute-start = (bf16[8,24,384]{2,1,0:T(8,128)(2,1)S(1)}, bf16[8,24,384]{2,1,0:T(8,128)(2,1)S(1)}, u32[]{:S(2)}, u32[]{:S(2)}) collective-permute-start(bf16[8,24,384]{2,1,0:T(8,128)(2,1)S(1)} %all-to-all-done), channel_id=1, source_target_pairs={{16,0},{504,8},{32,16},{8,24},{48,32},{24,40},{64,48},{40,56},{80,... | collective-permute-start | bytes 442376 | tf_op jit(solution)/shard_map/ppermute | solution.py:37
  71.1 7.7 %collective-permute-start.1 = (bf16[8,24,384]{2,1,0:T(8,128)(2,1)S(1)}, bf16[8,24,384]{2,1,0:T(8,128)(2,1)S(1)}, u32[]{:S(2)}, u32[]{:S(2)}) collective-permute-start(bf16[8,24,384]{2,1,0:T(8,128)(2,1)S(1)} %all-to-all-done), channel_id=1, source_target_pairs={{496,0},{24,8},{0,16},{40,24},{16,32},{56,40},{32,48},{72,56},{48,... | collective-permute-start | bytes 442376 | tf_op jit(solution)/shard_map/ppermute | solution.py:37
  74.5 8.3 %collective-permute-start.2 = (bf16[8,24,384]{2,1,0:T(8,128)(2,1)S(1)}, bf16[8,24,384]{2,1,0:T(8,128)(2,1)S(1)}, u32[]{:S(2)}, u32[]{:S(2)}) collective-permute-start(bf16[8,24,384]{2,1,0:T(8,128)(2,1)S(1)} %all-to-all-done), channel_id=1, source_target_pairs={{32,0},{488,8},{48,16},{504,24},{64,32},{8,40},{80,48},{24,56},{96... | collective-permute-start | bytes 442376 | tf_op jit(solution)/shard_map/ppermute | solution.py:37
  77.8 43.5 %copy-start.2 = (bf16[512,384]{1,0:T(8,128)(2,1)S(1)}, bf16[512,384]{1,0:T(8,128)(2,1)}, u32[]{:S(2)}) copy-start(bf16[512,384]{1,0:T(8,128)(2,1)} %param.5) | copy-start | bytes 1179652
  82.8 34.4 %collective-permute-start.3 = (bf16[8,4,24,384]{3,2,1,0:T(8,128)(2,1)S(1)}, bf16[8,4,24,384]{3,2,1,0:T(8,128)(2,1)S(1)}, u32[]{:S(2)}, u32[]{:S(2)}) collective-permute-start(bf16[8,4,24,384]{3,2,1,0:T(8,128)(2,1)S(1)} %bitcast_dynamic-update-slice_fusion.3), channel_id=1, source_target_pairs={{0,512},{8,520},{16,528},{24,536},{32,544},{40,552},{48,560},{56,5... | collective-permute-start | bytes 1769480 | tf_op jit(solution)/shard_map/ppermute | solution.py:63
  117.5 9.4 %collective-permute-start.4 = (bf16[2,8,4,24,384]{4,3,2,1,0:T(8,128)(2,1)S(1)}, bf16[2,8,4,24,384]{4,3,2,1,0:T(8,128)(2,1)}, u32[]{:S(2)}, u32[]{:S(2)}) collective-permute-start(bf16[2,8,4,24,384]{4,3,2,1,0:T(8,128)(2,1)S(1)} %maximum_select_fusion.1), channel_id=1, source_target_pairs={{0,8},{8,0},{16,24},{24,16},{32,40},{40,32},{48,56},{56,48},{64,72... | collective-permute-start | bytes 3538952 | tf_op jit(solution)/shard_map/ppermute | solution.py:66
  134.3 2.0 %copy-start = (f32[2,3,256,256]{2,3,1,0:T(8,128)S(1)}, f32[2,3,256,256]{2,3,1,0:T(8,128)}, u32[]{:S(2)}) copy-start(f32[2,3,256,256]{2,3,1,0:T(8,128)} %get-tuple-element.7) | copy-start | bytes 4718596
  134.4 2.0 %copy-start.1 = (bf16[2,256,3,128]{3,2,1,0:T(4,128)(2,1)S(1)}, bf16[2,256,3,128]{3,2,1,0:T(4,128)(2,1)}, u32[]{:S(2)}) copy-start(bf16[2,256,3,128]{3,2,1,0:T(4,128)(2,1)} %reshape.103) | copy-start | bytes 1179652

commit v2 on v0

v2 whole, which is shorter than its diff:
```python
import functools
import math

import jax
import jax.numpy as jnp
import numpy as np
from jax import lax
from jax.experimental import pallas as pl
from jax.experimental.pallas import tpu as pltpu
from jax.sharding import PartitionSpec as P

HEAD_SIZE = 128
PATCHES = 256
XLO, Z, CORES = 2, 32, 2
Y, XHI = 4, 2
STRIDE = 4
FAR = Z // STRIDE
HALVES = 2
QUADS = FAR // HALVES
VMEM = pl.BlockSpec(memory_space=pltpu.VMEM)
SMEM = pl.BlockSpec(memory_space=pltpu.SMEM)
NT = (((1,), (1,)), ((), ()))
TN = (((0,), (0,)), ((), ()))


def dp_index(x, z, c):
    return (x * Z + z % Z) * CORES + c


def everyone():
    return [(x, z, c) for x in range(XLO) for z in range(Z) for c in range(CORES)]


def gather_as_all_to_all(array, groups):
    many = jnp.broadcast_to(array[None], (len(groups[0]),) + array.shape)
    return lax.all_to_all(many, "dp", 0, 0, tiled=True, axis_index_groups=groups)


def far_rows(weight):
    groups = [
        [dp_index(x, r + STRIDE * k, c) for k in range(FAR)]
        for x in range(XLO)
        for r in range(STRIDE)
        for c in range(CORES)
    ]
    return gather_as_all_to_all(weight, groups)


def near_rows(far):
    groups = [
        [dp_index(x, STRIDE * k + r, c) for x in range(XLO) for r in range(STRIDE)]
        for k in range(FAR)
        for c in range(CORES)
    ]
    return gather_as_all_to_all(far, groups)


def core_swap(array):
    return lax.ppermute(
        array, "dp", [(dp_index(x, z, c), dp_index(x, z, 1 - c)) for x, z, c in everyone()]
    )


def arrange_columns(width):
    rows = width // (HALVES * STRIDE * CORES)
    order = (
        np.arange(width)
        .reshape(HALVES, STRIDE, CORES, rows)
        .transpose(2, 1, 0, 3)
        .reshape(width)
    )
    return jnp.asarray(np.arange(width)[:, None] == order[None, :], jnp.bfloat16)


def arrange_kernel(grad_ref, order_ref, out_ref):
    out_ref[...] = jnp.dot(
        grad_ref[...], order_ref[...], preferred_element_type=jnp.float32
    ).astype(out_ref.dtype)


def grad_shift(array, dy, dx):
    mp = Y * XHI
    pairs = []
    for d in range(XLO * Z * CORES):
        sign = 1 - 2 * (d % CORES)
        for y in range(Y):
            for h in range(XHI):
                source = ((y + sign * dy) % Y) * XHI + (h + dx) % XHI
                pairs.append((d * mp + source, d * mp + y * XHI + h))
    return lax.ppermute(array, ("dp", "mp"), pairs)


def arrange(grad):
    rows, width = grad.shape
    return pl.pallas_call(
        arrange_kernel,
        out_shape=jax.ShapeDtypeStruct(grad.shape, grad.dtype),
        in_specs=[VMEM, VMEM],
        out_specs=VMEM,
        name="arrange",
        cost_estimate=pl.CostEstimate(
            flops=2 * rows * width * width, bytes_accessed=6 * rows * width, transcendentals=0
        ),
    )(grad, arrange_columns(width))


def gather_both(weight, grad):
    far = far_rows(weight)
    arranged = arrange(grad)
    across = grad_shift(arranged, 0, 1)
    same = [grad_shift(arranged, dy, 0) for dy in (1, -1, 2)]
    far, across, *same = lax.optimization_barrier((far, across, *same))
    mine = near_rows(far)
    shifted = [grad_shift(across, dy, 0) for dy in (1, -1, 2)]
    mine, *shifted = lax.optimization_barrier((mine, *shifted))
    other = core_swap(mine)
    core = lax.axis_index("dp") & 1
    mp = lax.axis_index("mp")
    y, h, sign = mp >> 1, mp & 1, 1 - 2 * core
    places = [
        (((y + sign * dy) & 3) << 1) | side for side in (h, 1 - h) for dy in (0, 1, -1, 2)
    ]
    places = jnp.stack(places + [core]).astype(jnp.int32)
    return mine, other, [arranged, *same, across, *shifted], places


def probs_kernel(images, heads, query_ref, key_ref, probs_ref):
    scale = 1.0 / math.sqrt(HEAD_SIZE)
    for image in range(images):
        rows = pl.ds(image * PATCHES, PATCHES)
        for head in range(heads):
            cols = pl.ds(head * HEAD_SIZE, HEAD_SIZE)
            scores = (
                lax.dot_general(
                    key_ref[rows, cols],
                    query_ref[rows, cols],
                    NT,
                    preferred_element_type=jnp.float32,
                )
                * scale
            )
            exped = jnp.exp(scores - jnp.max(scores, axis=0, keepdims=True))
            probs_ref[image * heads + head] = exped / jnp.sum(exped, axis=0, keepdims=True)


def tail_kernel(
    images, heads, place_ref, mine_ref, across_ref, probs_ref, query_ref, key_ref, value_ref, *rest
):
    blocks, (dq_ref, dk_ref, dv_ref, weight_ref) = rest[: Y * XHI], rest[Y * XHI :]
    scale = 1.0 / math.sqrt(HEAD_SIZE)
    group = mine_ref.shape[3]
    core = place_ref[8]
    for source, c in ((mine_ref, core), (across_ref, 1 - core)):
        for r in range(STRIDE):
            start = pl.multiple_of((c * STRIDE + r) * group, 16)
            for x in range(XLO):
                for q in range(QUADS):
                    weight_ref[x * QUADS + q, pl.ds(start, group), :] = source[x, r, q]
    for image in range(images):
        rows = pl.ds(image * PATCHES, PATCHES)
        total = None
        for p, block in enumerate(blocks):
            product = jnp.dot(
                block[rows, :], weight_ref[place_ref[p]], preferred_element_type=jnp.float32
            )
            total = product if total is None else total + product
        grad_image = total.astype(jnp.bfloat16)
        for head in range(heads):
            cols = pl.ds(head * HEAD_SIZE, HEAD_SIZE)
            grad = grad_image[:, head * HEAD_SIZE : (head + 1) * HEAD_SIZE]
            probs = probs_ref[image * heads + head]
            dv_ref[rows, cols] = jnp.dot(
                probs.astype(jnp.bfloat16), grad, preferred_element_type=jnp.float32
            ).astype(dv_ref.dtype)
            d_probs = lax.dot_general(
                value_ref[rows, cols], grad, NT, preferred_element_type=jnp.float32
            )
            row_dot = jnp.sum(probs * d_probs, axis=0, keepdims=True)
            d_scores = (probs * (d_probs - row_dot)).astype(jnp.bfloat16)
            dk_ref[rows, cols] = (
                jnp.dot(d_scores, query_ref[rows, cols], preferred_element_type=jnp.float32)
                * scale
            ).astype(dk_ref.dtype)
            dq_ref[rows, cols] = (
                lax.dot_general(
                    d_scores, key_ref[rows, cols], TN, preferred_element_type=jnp.float32
                )
                * scale
            ).astype(dq_ref.dtype)


def body(queries, keys, values, grad_out, out_weight):
    tok_rows, width = queries.shape
    images, heads = tok_rows // PATCHES, width // HEAD_SIZE
    mine, other, blocks, places = gather_both(out_weight, grad_out)
    probs = pl.pallas_call(
        functools.partial(probs_kernel, images, heads),
        out_shape=jax.ShapeDtypeStruct((images * heads, PATCHES, PATCHES), jnp.float32),
        in_specs=[VMEM, VMEM],
        out_specs=VMEM,
        name="probs",
        cost_estimate=pl.CostEstimate(
            flops=2 * tok_rows * PATCHES * width,
            bytes_accessed=4 * tok_rows * width + 4 * heads * tok_rows * PATCHES,
            transcendentals=heads * tok_rows * PATCHES,
        ),
        compiler_params=pltpu.CompilerParams(vmem_limit_bytes=16 << 20),
    )(queries, keys)
    pieces = (XLO, STRIDE, QUADS, HALVES * out_weight.shape[0], width)
    like = jax.ShapeDtypeStruct(queries.shape, queries.dtype)
    return pl.pallas_call(
        functools.partial(tail_kernel, images, heads),
        out_shape=(like, like, like),
        in_specs=[SMEM] + [VMEM] * 14,
        out_specs=(VMEM, VMEM, VMEM),
        scratch_shapes=[pltpu.VMEM((XLO * QUADS, width, width), jnp.bfloat16)],
        name="tail",
        cost_estimate=pl.CostEstimate(
            flops=2 * tok_rows * width * (8 * width + 4 * PATCHES),
            bytes_accessed=2 * (15 * tok_rows * width + 8 * width * width),
            transcendentals=0,
        ),
        compiler_params=pltpu.CompilerParams(vmem_limit_bytes=16 << 20),
    )(
        places,
        mine.reshape(pieces),
        other.reshape(pieces),
        probs,
        queries,
        keys,
        values,
        *blocks,
    )


def solution(mesh):
    placed = (P("dp", "mp"), P("dp", "mp"), P("dp", "mp"), P("dp", "mp"), P("dp", "mp"))
    return jax.shard_map(
        body,
        mesh=mesh,
        in_specs=placed,
        out_specs=(P("dp", "mp"), P("dp", "mp"), P("dp", "mp")),
        check_vma=False,
    )
```

time: 371 us -> 110 us (0.30)
  waiting for transfers between devices: 342 us -> 25 us
  starting transfers between devices: 0.08 us -> 66.2 us
  between operations: 14.2 us -> 0.84 us
  Pallas kernels: 0 us -> 8.98 us
  matrix products: 7.69 us -> 0 us
    all_gather x2 -> x0, waiting for transfers between devices: 340 us -> none  [the longest x1 244 us: body(): full_weight = lax.all_gather(out_weight, 'dp', axis=0, tiled=True)]
    all_to_all x0 -> x2, starting transfers between devices: none -> 37.2 us  [gather_as_all_to_all(): lax.all_to_all(many, 'dp', 0, 0, tiled=True, axis_index_groups=groups)]
    ppermute x0 -> x8, starting transfers between devices: none -> 29 us  [the longest x7 24.8 us: grad_shift(): return lax.ppermute(array, ('dp', 'mp'), pairs)]
    ppermute x0 -> x8, waiting for transfers between devices: none -> 20.2 us  [the longest x7 18.7 us: grad_shift(): return lax.ppermute(array, ('dp', 'mp'), pairs)]
    pallas_call x0 -> x3, Pallas kernels: none -> 8.98 us  [the longest x1 6.03 us: body(): pl.pallas_call(functools.partial(tail_kernel, images, heads), out_shape=(...]
    dot_general x5 -> x0, matrix products: 7.04 us -> none  [the longest x1 4.4 us: body(): jnp.dot(whole_grad, full_weight, preferred_element_type=jnp.float32)]
    all_to_all x0 -> x2, waiting for transfers between devices: none -> 4.76 us  [gather_as_all_to_all(): lax.all_to_all(many, 'dp', 0, 0, tiled=True, axis_index_groups=groups)]
  transfers between devices with their start and end apart: 2 -> 10, of which waited for: 2 -> 8; matrix products, arithmetic and copies ran while one was open for 1% -> 0% of each run, Pallas kernels for 0% -> 3%
where the time goes in v2:
time: 110 us
  starting transfers between devices  66.2 us (60%)
  waiting for transfers between devices  25 us (23%)
  Pallas kernels  8.98 us (8%)
  local copies, waits for them, and re-layouts  8.51 us (8%)
    all_to_all x2, starting transfers between devices, gather_as_all_to_all(): lax.all_to_all(many, 'dp', 0, 0, tiled=True, axis_index_groups=groups)  37.2 us
    ppermute x7, starting transfers between devices, grad_shift(): return lax.ppermute(array, ('dp', 'mp'), pairs)  24.8 us
    ppermute x7, waiting for transfers between devices, grad_shift(): return lax.ppermute(array, ('dp', 'mp'), pairs)  18.7 us
    pallas_call x1, Pallas kernels, body(): pl.pallas_call(functools.partial(tail_kernel, images, heads), out_shape=(...  6.03 us
    unnamed x32, local copies, waits for them, and re-layouts  5.83 us
    all_to_all x2, waiting for transfers between devices, gather_as_all_to_all(): lax.all_to_all(many, 'dp', 0, 0, tiled=True, axis_index_groups=groups)  4.76 us
    ppermute x1, starting transfers between devices, core_swap(): lax.ppermute(array, 'dp', [(dp_index(x, z, c), dp_index(x, z, 1 - c)) for...  4.19 us
    broadcast_in_dim x2, local copies, waits for them, and re-layouts, gather_as_all_to_all(): many = jnp.broadcast_to(array[None], (len(groups[0]),) + array.shape)  2.6 us
  transfers between devices with their start and end apart: 10, of which 8 were waited for; matrix products, arithmetic and copies ran while one was open for 0% of the time, Pallas kernels for 3%

profile of v2, /device:TPU:1, one launch (start us, length us, event | category | flops | bytes accessed | tf_op | source)
XLA Modules:
  0.0 109.5 jit_solution(14491302398470189107)
XLA Ops:
  0.6 1.4 %broadcast_in_dim.4 = bf16[8,24,384]{2,1,0:T(8,128)(2,1)} broadcast(bf16[24,384]{1,0:T(8,128)(2,1)} %param.10), dimensions={1,2} | broadcast | bytes 165888 | tf_op jit(solution)/shard_map/broadcast_in_dim | solution.py:35
  2.0 28.9 %all-to-all-start = ((bf16[8,24,384]{2,1,0:T(8,128)(2,1)}), bf16[8,24,384]{2,1,0:T(8,128)(2,1)S(1)}, u32[]{:S(2)}, u32[]{:S(2)}) async-start(bf16[8,24,384]{2,1,0:T(8,128)(2,1)} %broadcast_in_dim.4), calls=%async_computation | async-start | bytes 294912 | tf_op jit(solution)/shard_map/all_to_all | solution.py:36
  30.9 2.2 %arrange.1.rest_0_ = bf16[512,384]{1,0:T(8,128)(2,1)} custom-call(bf16[512,384]{1,0:T(8,128)(2,1)} %grad_ref.1, bf16[384,384]{1,0:T(8,128)(2,1)} %constant.19.clone.order_ref), custom_call_target="tpu_custom_call" | custom-call | flops 150994944 | bytes 1179648 | tf_op jit(solution)/shard_map/arrange/pallas_call | solution.py:95
  33.1 4.8 %collective-permute-start.3 = (bf16[512,384]{1,0:T(8,128)(2,1)}, bf16[512,384]{1,0:T(8,128)(2,1)S(1)}, u32[]{:S(2)}, u32[]{:S(2)}) collective-permute-start(bf16[512,384]{1,0:T(8,128)(2,1)} %arrange.1.rest_0_), channel_id=1, source_target_pairs={{4,0},{5,1},{6,2},{7,3},{0,4},{1,5},{2,6},{3,7},{12,8},{13,9},{14,... | collective-permute-start | bytes 1179656 | tf_op jit(solution)/shard_map/ppermute | solution.py:90
  38.0 2.7 %collective-permute-start.2 = (bf16[512,384]{1,0:T(8,128)(2,1)}, bf16[512,384]{1,0:T(8,128)(2,1)S(1)}, u32[]{:S(2)}, u32[]{:S(2)}) collective-permute-start(bf16[512,384]{1,0:T(8,128)(2,1)} %arrange.1.rest_0_), channel_id=1, source_target_pairs={{6,0},{7,1},{0,2},{1,3},{2,4},{3,5},{4,6},{5,7},{10,8},{11,9},{12,... | collective-permute-start | bytes 1179656 | tf_op jit(solution)/shard_map/ppermute | solution.py:90
  40.6 2.6 %collective-permute-start.1 = (bf16[512,384]{1,0:T(8,128)(2,1)}, bf16[512,384]{1,0:T(8,128)(2,1)S(1)}, u32[]{:S(2)}, u32[]{:S(2)}) collective-permute-start(bf16[512,384]{1,0:T(8,128)(2,1)} %arrange.1.rest_0_), channel_id=1, source_target_pairs={{2,0},{3,1},{4,2},{5,3},{6,4},{7,5},{0,6},{1,7},{14,8},{15,9},{8,1... | collective-permute-start | bytes 1179656 | tf_op jit(solution)/shard_map/ppermute | solution.py:90
  43.3 4.7 %collective-permute-start = (bf16[512,384]{1,0:T(8,128)(2,1)}, bf16[512,384]{1,0:T(8,128)(2,1)S(1)}, u32[]{:S(2)}, u32[]{:S(2)}) collective-permute-start(bf16[512,384]{1,0:T(8,128)(2,1)} %arrange.1.rest_0_), channel_id=1, source_target_pairs={{1,0},{0,1},{3,2},{2,3},{5,4},{4,5},{7,6},{6,7},{9,8},{8,9},{11,10... | collective-permute-start | bytes 1179656 | tf_op jit(solution)/shard_map/ppermute | solution.py:90
  47.9 7.3 %collective-permute-done.2.rest_2_ = bf16[512,384]{1,0:T(8,128)(2,1)S(1)} collective-permute-done((bf16[512,384]{1,0:T(8,128)(2,1)}, bf16[512,384]{1,0:T(8,128)(2,1)S(1)}, u32[]{:S(2)}, u32[]{:S(2)}) %collective-permute-start.2) | collective-permute-done | bytes 393248 | tf_op jit(solution)/shard_map/ppermute | solution.py:90
  55.2 0.7 copy-done.4
  56.0 0.3 collective-permute-done.1.rest_1_
  56.3 0.7 copy-done.6
  57.0 0.2 all-to-all-done
  57.2 1.2 %broadcast_in_dim.5 = bf16[8,8,24,384]{3,2,1,0:T(8,128)(2,1)} broadcast(bf16[8,24,384]{2,1,0:T(8,128)(2,1)S(1)} %all-to-all-done), dimensions={1,2,3} | broadcast | bytes 1327104 | tf_op jit(solution)/shard_map/broadcast_in_dim | solution.py:35
  58.4 8.3 %all-to-all-start.1 = ((bf16[8,8,24,384]{3,2,1,0:T(8,128)(2,1)}), bf16[8,8,24,384]{3,2,1,0:T(8,128)(2,1)S(1)}, u32[]{:S(2)}, u32[]{:S(2)}) async-start(bf16[8,8,24,384]{3,2,1,0:T(8,128)(2,1)} %broadcast_in_dim.5), calls=%async_computation.1 | async-start | bytes 2359296 | tf_op jit(solution)/shard_map/all_to_all | solution.py:36
  66.7 4.8 %collective-permute-start.6 = (bf16[512,384]{1,0:T(8,128)(2,1)S(1)}, bf16[512,384]{1,0:T(8,128)(2,1)S(1)}, u32[]{:S(2)}, u32[]{:S(2)}) collective-permute-start(bf16[512,384]{1,0:T(8,128)(2,1)S(1)} %collective-permute-done.rest_4_), channel_id=1, source_target_pairs={{4,0},{5,1},{6,2},{7,3},{0,4},{1,5},{2,6},{3,7},{12,8},{13,9},{14,... | collective-permute-start | bytes 1179656 | tf_op jit(solution)/shard_map/ppermute | solution.py:90
  71.5 2.7 %collective-permute-start.5 = (bf16[512,384]{1,0:T(8,128)(2,1)S(1)}, bf16[512,384]{1,0:T(8,128)(2,1)S(1)}, u32[]{:S(2)}, u32[]{:S(2)}) collective-permute-start(bf16[512,384]{1,0:T(8,128)(2,1)S(1)} %collective-permute-done.rest_4_), channel_id=1, source_target_pairs={{6,0},{7,1},{0,2},{1,3},{2,4},{3,5},{4,6},{5,7},{10,8},{11,9},{12,... | collective-permute-start | bytes 1179656 | tf_op jit(solution)/shard_map/ppermute | solution.py:90
  74.2 2.6 %collective-permute-start.4 = (bf16[512,384]{1,0:T(8,128)(2,1)S(1)}, bf16[512,384]{1,0:T(8,128)(2,1)S(1)}, u32[]{:S(2)}, u32[]{:S(2)}) collective-permute-start(bf16[512,384]{1,0:T(8,128)(2,1)S(1)} %collective-permute-done.rest_4_), channel_id=1, source_target_pairs={{2,0},{3,1},{4,2},{5,3},{6,4},{7,5},{0,6},{1,7},{14,8},{15,9},{8,1... | collective-permute-start | bytes 1179656 | tf_op jit(solution)/shard_map/ppermute | solution.py:90
  76.8 2.8 %collective-permute-done.6.rest_7_ = bf16[512,384]{1,0:T(8,128)(2,1)S(1)} collective-permute-done((bf16[512,384]{1,0:T(8,128)(2,1)S(1)}, bf16[512,384]{1,0:T(8,128)(2,1)S(1)}, u32[]{:S(2)}, u32[]{:S(2)}) %collective-permute-start.6) | collective-permute-done | bytes 393248 | tf_op jit(solution)/shard_map/ppermute | solution.py:90
  79.6 0.8 copy-done.10
  80.4 8.0 %collective-permute-done.5.rest_6_ = bf16[512,384]{1,0:T(8,128)(2,1)S(1)} collective-permute-done((bf16[512,384]{1,0:T(8,128)(2,1)S(1)}, bf16[512,384]{1,0:T(8,128)(2,1)S(1)}, u32[]{:S(2)}, u32[]{:S(2)}) %collective-permute-start.5) | collective-permute-done | bytes 393248 | tf_op jit(solution)/shard_map/ppermute | solution.py:90
  88.4 0.7 copy-done.12
  89.2 0.3 collective-permute-done.4.rest_5_
  89.5 0.8 copy-done.14
  90.2 4.6 %all-to-all-done.1 = bf16[8,8,24,384]{3,2,1,0:T(8,128)(2,1)S(1)} async-done(((bf16[8,8,24,384]{3,2,1,0:T(8,128)(2,1)}), bf16[8,8,24,384]{3,2,1,0:T(8,128)(2,1)S(1)}, u32[]{:S(2)}, u32[]{:S(2)}) %all-to-all-start.1) | async-done | bytes 1179680 | tf_op jit(solution)/shard_map/all_to_all | solution.py:36
  94.8 4.2 %collective-permute-start.7 = (bf16[8,8,24,384]{3,2,1,0:T(8,128)(2,1)S(1)}, bf16[8,8,24,384]{3,2,1,0:T(8,128)(2,1)S(1)}, u32[]{:S(2)}, u32[]{:S(2)}) collective-permute-start(bf16[8,8,24,384]{3,2,1,0:T(8,128)(2,1)S(1)} %all-to-all-done.1), channel_id=1, source_target_pairs={{0,8},{8,0},{16,24},{24,16},{32,40},{40,32},{48,56},{56,48},{64,72... | collective-permute-start | bytes 3538952 | tf_op jit(solution)/shard_map/ppermute | solution.py:59
  99.0 0.1 stack.39.place_ref
  99.1 0.0 copy-start.5
  99.2 0.7 probs.1.probs_ref
  99.9 1.5 %collective-permute-done.7 = bf16[8,8,24,384]{3,2,1,0:T(8,128)(2,1)S(1)} collective-permute-done((bf16[8,8,24,384]{3,2,1,0:T(8,128)(2,1)S(1)}, bf16[8,8,24,384]{3,2,1,0:T(8,128)(2,1)S(1)}, u32[]{:S(2)}, u32[]{:S(2)}) %collective-permute-start.7) | collective-permute-done | bytes 1179680 | tf_op jit(solution)/shard_map/ppermute | solution.py:59
  101.5 1.0 copy-done.13
  102.5 1.0 copy-done.15
  103.5 6.0 %tail.1 = (bf16[512,384]{1,0:T(8,128)(2,1)}, bf16[512,384]{1,0:T(8,128)(2,1)}, bf16[512,384]{1,0:T(8,128)(2,1)}) custom-call(s32[9]{0:T(128)S(1)} %stack.39.place_ref, bf16[2,4,4,48,384]{4,3,2,1,0:T(8,128)(2,1)S(1)} %bitcast.11, bf16[2,4,4,48,384]{4,3,2,1,0:T(8,128)(2,1)S(1)} %bitcast.12, f32[6,256,256]{2,1,0:T(8,128)S(1)} %probs.1.probs_ref, ...), custom_call_target="tpu_custom_call" | custom-call | flops 1610612736 | bytes 8257536 | tf_op jit(solution)/shard_map/tail/pallas_call | solution.py:211
  (26 shorter events, 0.1 us)
Async XLA Ops:
  2.0 55.2 %all-to-all-start = ((bf16[8,24,384]{2,1,0:T(8,128)(2,1)}), bf16[8,24,384]{2,1,0:T(8,128)(2,1)S(1)}, u32[]{:S(2)}, u32[]{:S(2)}) async-start(bf16[8,24,384]{2,1,0:T(8,128)(2,1)} %broadcast_in_dim.4), calls=%async_computation | async-start | bytes 294912 | tf_op jit(solution)/shard_map/all_to_all | solution.py:36
  33.1 14.8 %collective-permute-start.3 = (bf16[512,384]{1,0:T(8,128)(2,1)}, bf16[512,384]{1,0:T(8,128)(2,1)S(1)}, u32[]{:S(2)}, u32[]{:S(2)}) collective-permute-start(bf16[512,384]{1,0:T(8,128)(2,1)} %arrange.1.rest_0_), channel_id=1, source_target_pairs={{4,0},{5,1},{6,2},{7,3},{0,4},{1,5},{2,6},{3,7},{12,8},{13,9},{14,... | collective-permute-start | bytes 1179656 | tf_op jit(solution)/shard_map/ppermute | solution.py:90
  38.0 17.2 %collective-permute-start.2 = (bf16[512,384]{1,0:T(8,128)(2,1)}, bf16[512,384]{1,0:T(8,128)(2,1)S(1)}, u32[]{:S(2)}, u32[]{:S(2)}) collective-permute-start(bf16[512,384]{1,0:T(8,128)(2,1)} %arrange.1.rest_0_), channel_id=1, source_target_pairs={{6,0},{7,1},{0,2},{1,3},{2,4},{3,5},{4,6},{5,7},{10,8},{11,9},{12,... | collective-permute-start | bytes 1179656 | tf_op jit(solution)/shard_map/ppermute | solution.py:90
  40.6 15.6 %collective-permute-start.1 = (bf16[512,384]{1,0:T(8,128)(2,1)}, bf16[512,384]{1,0:T(8,128)(2,1)S(1)}, u32[]{:S(2)}, u32[]{:S(2)}) collective-permute-start(bf16[512,384]{1,0:T(8,128)(2,1)} %arrange.1.rest_0_), channel_id=1, source_target_pairs={{2,0},{3,1},{4,2},{5,3},{6,4},{7,5},{0,6},{1,7},{14,8},{15,9},{8,1... | collective-permute-start | bytes 1179656 | tf_op jit(solution)/shard_map/ppermute | solution.py:90
  43.3 13.8 %collective-permute-start = (bf16[512,384]{1,0:T(8,128)(2,1)}, bf16[512,384]{1,0:T(8,128)(2,1)S(1)}, u32[]{:S(2)}, u32[]{:S(2)}) collective-permute-start(bf16[512,384]{1,0:T(8,128)(2,1)} %arrange.1.rest_0_), channel_id=1, source_target_pairs={{1,0},{0,1},{3,2},{2,3},{5,4},{4,5},{7,6},{6,7},{9,8},{8,9},{11,10... | collective-permute-start | bytes 1179656 | tf_op jit(solution)/shard_map/ppermute | solution.py:90
  55.2 0.7 copy-start.4
  56.3 0.7 copy-start.6
  57.0 17.2 %copy-start.8 = (bf16[512,384]{1,0:T(8,128)(2,1)}, bf16[512,384]{1,0:T(8,128)(2,1)S(1)}, u32[]{:S(2)}) copy-start(bf16[512,384]{1,0:T(8,128)(2,1)S(1)} %collective-permute-done.rest_4_) | copy-start | bytes 1179652
  58.4 40.7 %copy-start = (bf16[512,384]{1,0:T(8,128)(2,1)S(1)}, bf16[512,384]{1,0:T(8,128)(2,1)}, u32[]{:S(2)}) copy-start(bf16[512,384]{1,0:T(8,128)(2,1)} %query_ref.3) | copy-start | bytes 1179652
  58.4 40.7 %copy-start.1 = (bf16[512,384]{1,0:T(8,128)(2,1)S(1)}, bf16[512,384]{1,0:T(8,128)(2,1)}, u32[]{:S(2)}) copy-start(bf16[512,384]{1,0:T(8,128)(2,1)} %key_ref.3) | copy-start | bytes 1179652
  58.4 36.4 %all-to-all-start.1 = ((bf16[8,8,24,384]{3,2,1,0:T(8,128)(2,1)}), bf16[8,8,24,384]{3,2,1,0:T(8,128)(2,1)S(1)}, u32[]{:S(2)}, u32[]{:S(2)}) async-start(bf16[8,8,24,384]{3,2,1,0:T(8,128)(2,1)} %broadcast_in_dim.5), calls=%async_computation.1 | async-start | bytes 2359296 | tf_op jit(solution)/shard_map/all_to_all | solution.py:36
  66.7 12.9 %collective-permute-start.6 = (bf16[512,384]{1,0:T(8,128)(2,1)S(1)}, bf16[512,384]{1,0:T(8,128)(2,1)S(1)}, u32[]{:S(2)}, u32[]{:S(2)}) collective-permute-start(bf16[512,384]{1,0:T(8,128)(2,1)S(1)} %collective-permute-done.rest_4_), channel_id=1, source_target_pairs={{4,0},{5,1},{6,2},{7,3},{0,4},{1,5},{2,6},{3,7},{12,8},{13,9},{14,... | collective-permute-start | bytes 1179656 | tf_op jit(solution)/shard_map/ppermute | solution.py:90
  71.5 16.9 %collective-permute-start.5 = (bf16[512,384]{1,0:T(8,128)(2,1)S(1)}, bf16[512,384]{1,0:T(8,128)(2,1)S(1)}, u32[]{:S(2)}, u32[]{:S(2)}) collective-permute-start(bf16[512,384]{1,0:T(8,128)(2,1)S(1)} %collective-permute-done.rest_4_), channel_id=1, source_target_pairs={{6,0},{7,1},{0,2},{1,3},{2,4},{3,5},{4,6},{5,7},{10,8},{11,9},{12,... | collective-permute-start | bytes 1179656 | tf_op jit(solution)/shard_map/ppermute | solution.py:90
  74.2 15.2 %collective-permute-start.4 = (bf16[512,384]{1,0:T(8,128)(2,1)S(1)}, bf16[512,384]{1,0:T(8,128)(2,1)S(1)}, u32[]{:S(2)}, u32[]{:S(2)}) collective-permute-start(bf16[512,384]{1,0:T(8,128)(2,1)S(1)} %collective-permute-done.rest_4_), channel_id=1, source_target_pairs={{2,0},{3,1},{4,2},{5,3},{6,4},{7,5},{0,6},{1,7},{14,8},{15,9},{8,1... | collective-permute-start | bytes 1179656 | tf_op jit(solution)/shard_map/ppermute | solution.py:90
  79.6 0.8 copy-start.10
  88.4 0.7 copy-start.12
  89.4 0.8 copy-start.14
  94.8 6.6 %collective-permute-start.7 = (bf16[8,8,24,384]{3,2,1,0:T(8,128)(2,1)S(1)}, bf16[8,8,24,384]{3,2,1,0:T(8,128)(2,1)S(1)}, u32[]{:S(2)}, u32[]{:S(2)}) collective-permute-start(bf16[8,8,24,384]{3,2,1,0:T(8,128)(2,1)S(1)} %all-to-all-done.1), channel_id=1, source_target_pairs={{0,8},{8,0},{16,24},{24,16},{32,40},{40,32},{48,56},{56,48},{64,72... | collective-permute-start | bytes 3538952 | tf_op jit(solution)/shard_map/ppermute | solution.py:59
  99.1 2.3 %copy-start.2 = (bf16[512,384]{1,0:T(8,128)(2,1)S(1)}, bf16[512,384]{1,0:T(8,128)(2,1)}, u32[]{:S(2)}) copy-start(bf16[512,384]{1,0:T(8,128)(2,1)} %arrange.1.rest_0_) | copy-start | bytes 1179652
  99.1 2.3 %copy-start.3 = (bf16[512,384]{1,0:T(8,128)(2,1)S(1)}, bf16[512,384]{1,0:T(8,128)(2,1)}, u32[]{:S(2)}) copy-start(bf16[512,384]{1,0:T(8,128)(2,1)} %value_ref.1) | copy-start | bytes 1179652
  99.1 2.3 %copy-start.5 = (bf16[512,384]{1,0:T(8,128)(2,1)S(1)}, bf16[512,384]{1,0:T(8,128)(2,1)}, u32[]{:S(2)}) copy-start(bf16[512,384]{1,0:T(8,128)(2,1)} %copy-done.4) | copy-start | bytes 1179652
  99.2 2.3 %copy-start.7 = (bf16[512,384]{1,0:T(8,128)(2,1)S(1)}, bf16[512,384]{1,0:T(8,128)(2,1)}, u32[]{:S(2)}) copy-start(bf16[512,384]{1,0:T(8,128)(2,1)} %copy-done.6) | copy-start | bytes 1179652
  99.2 2.3 %copy-start.9 = (bf16[512,384]{1,0:T(8,128)(2,1)S(1)}, bf16[512,384]{1,0:T(8,128)(2,1)}, u32[]{:S(2)}) copy-start(bf16[512,384]{1,0:T(8,128)(2,1)} %copy-done.8) | copy-start | bytes 1179652
  99.2 2.3 %copy-start.11 = (bf16[512,384]{1,0:T(8,128)(2,1)S(1)}, bf16[512,384]{1,0:T(8,128)(2,1)}, u32[]{:S(2)}) copy-start(bf16[512,384]{1,0:T(8,128)(2,1)} %copy-done.10) | copy-start | bytes 1179652
  101.5 1.0 copy-start.13
  102.5 1.0 copy-start.15

commit v3 on v2

v3 whole, which is shorter than its diff:
```python
import functools
import math

import jax
import jax.numpy as jnp
import numpy as np
from jax import lax
from jax.experimental import pallas as pl
from jax.experimental.pallas import tpu as pltpu
from jax.sharding import PartitionSpec as P

HEAD_SIZE = 128
PATCHES = 256
XLO, Z, CORES = 2, 32, 2
Y, XHI = 4, 2
STRIDE = 4
FAR = Z // STRIDE
HALVES = 2
QUADS = FAR // HALVES
VMEM = pl.BlockSpec(memory_space=pltpu.VMEM)
ANY = pl.BlockSpec(memory_space=pl.ANY)
SMEM = pl.BlockSpec(memory_space=pltpu.SMEM)
NT = (((1,), (1,)), ((), ()))
TN = (((0,), (0,)), ((), ()))


def dp_index(x, z, c):
    return (x * Z + z % Z) * CORES + c


def everyone():
    return [(x, z, c) for x in range(XLO) for z in range(Z) for c in range(CORES)]


def far_rows(weight):
    groups = [
        [dp_index(x, r + STRIDE * k, c) for k in range(FAR)]
        for x in range(XLO)
        for r in range(STRIDE)
        for c in range(CORES)
    ]
    return lax.all_gather(weight, "dp", axis_index_groups=groups)


def z_shift(array, step):
    pairs = [
        (dp_index(x, z + (1 - 2 * c) * step, c), dp_index(x, z, c)) for x, z, c in everyone()
    ]
    return lax.ppermute(array, "dp", pairs)


def x_swap(array):
    return lax.ppermute(
        array, "dp", [(dp_index(x, z, c), dp_index(1 - x, z, c)) for x, z, c in everyone()]
    )


def core_swap(array):
    return lax.ppermute(
        array, "dp", [(dp_index(x, z, c), dp_index(x, z, 1 - c)) for x, z, c in everyone()]
    )


def arrange_columns(width):
    rows = width // (HALVES * STRIDE * CORES)
    order = (
        np.arange(width)
        .reshape(HALVES, STRIDE, CORES, rows)
        .transpose(2, 1, 0, 3)
        .reshape(width)
    )
    return jnp.asarray(np.arange(width)[:, None] == order[None, :], jnp.bfloat16)


def arrange_kernel(grad_ref, order_ref, out_ref, held, sems):
    held[...] = jnp.dot(
        grad_ref[...], order_ref[...], preferred_element_type=jnp.float32
    ).astype(held.dtype)
    copies = [
        pltpu.make_async_copy(held, out_ref.at[p], sems.at[p]) for p in range(out_ref.shape[0])
    ]
    for copy in copies:
        copy.start()
    for copy in copies:
        copy.wait()


def arranged_copies(grad, count):
    rows, width = grad.shape
    return pl.pallas_call(
        arrange_kernel,
        out_shape=jax.ShapeDtypeStruct((count, rows, width), grad.dtype),
        in_specs=[VMEM, VMEM],
        out_specs=ANY,
        scratch_shapes=[
            pltpu.VMEM((rows, width), grad.dtype),
            pltpu.SemaphoreType.DMA((count,)),
        ],
        name="arrange",
        cost_estimate=pl.CostEstimate(
            flops=2 * rows * width * width,
            bytes_accessed=2 * (count + 1) * rows * width,
            transcendentals=0,
        ),
    )(grad, arrange_columns(width))


STEPS = (0, 2, 1, -1)


def gather_both(weight, grad):
    rows, width = weight.shape
    blocks = lax.all_to_all(arranged_copies(grad, Y * XHI), "mp", 0, 0, tiled=True)
    far = far_rows(weight)
    both = jnp.stack([far, x_swap(far)])
    both, blocks = lax.optimization_barrier((both, blocks))
    mine = [z_shift(both, step) if step else both for step in STEPS]
    pieces = mine + [core_swap(piece) for piece in mine]
    pieces = [
        piece.reshape(XLO, QUADS, HALVES * rows, width) for piece in pieces
    ]
    here = lax.axis_index("dp")
    core, z, x = here & 1, (here >> 1) & (Z - 1), here >> 6
    residues = [
        (z + (1 - 2 * c) * step) & (STRIDE - 1) for c in (core, 1 - core) for step in STEPS
    ]
    places = jnp.stack(residues + [core, x]).astype(jnp.int32)
    return places, blocks, pieces


def tail_kernel(images, heads, place_ref, queries, keys, values, blocks, *rest):
    pieces, (dq_ref, dk_ref, dv_ref), scratch = rest[:8], rest[8:11], rest[11:]
    query_ref, key_ref, value_ref, blocks_ref, weight_ref, probs_ref, sems = scratch
    scale = 1.0 / math.sqrt(HEAD_SIZE)
    group = pieces[0].shape[2]
    count = XLO * QUADS
    core, here = place_ref[8], place_ref[9]
    copies = [(queries, query_ref), (keys, key_ref)]
    for p, piece in enumerate(pieces):
        c = core if p < 4 else 1 - core
        start = pl.multiple_of((c * STRIDE + place_ref[p]) * group, 16)
        for away in range(XLO):
            x = here if away == 0 else 1 - here
            there = weight_ref.at[pl.ds(x * QUADS, QUADS), pl.ds(start, group)]
            copies.append((piece.at[away], there))
    copies += [(blocks.at[j], blocks_ref.at[j]) for j in range(count)]
    copies.append((values, value_ref))
    copies = [pltpu.make_async_copy(*pair, sems.at[i]) for i, pair in enumerate(copies)]
    for copy in copies:
        copy.start()
    for copy in copies[:2]:
        copy.wait()
    for image in range(images):
        rows = pl.ds(image * PATCHES, PATCHES)
        for head in range(heads):
            cols = pl.ds(head * HEAD_SIZE, HEAD_SIZE)
            scores = (
                lax.dot_general(
                    key_ref[rows, cols],
                    query_ref[rows, cols],
                    NT,
                    preferred_element_type=jnp.float32,
                )
                * scale
            )
            exped = jnp.exp(scores - jnp.max(scores, axis=0, keepdims=True))
            probs_ref[image * heads + head] = exped / jnp.sum(exped, axis=0, keepdims=True)
    for copy in copies[2:18]:
        copy.wait()
    for image in range(images):
        rows = pl.ds(image * PATCHES, PATCHES)
        total = None
        for j in range(count):
            if image == 0:
                copies[18 + j].wait()
            product = jnp.dot(
                blocks_ref[j, rows, :], weight_ref[j], preferred_element_type=jnp.float32
            )
            total = product if total is None else total + product
        if image == 0:
            copies[-1].wait()
        grad_image = total.astype(jnp.bfloat16)
        for head in range(heads):
            cols = pl.ds(head * HEAD_SIZE, HEAD_SIZE)
            grad = grad_image[:, head * HEAD_SIZE : (head + 1) * HEAD_SIZE]
            probs = probs_ref[image * heads + head]
            dv_ref[rows, cols] = jnp.dot(
                probs.astype(jnp.bfloat16), grad, preferred_element_type=jnp.float32
            ).astype(dv_ref.dtype)
            d_probs = lax.dot_general(
                value_ref[rows, cols], grad, NT, preferred_element_type=jnp.float32
            )
            row_dot = jnp.sum(probs * d_probs, axis=0, keepdims=True)
            d_scores = (probs * (d_probs - row_dot)).astype(jnp.bfloat16)
            dk_ref[rows, cols] = (
                jnp.dot(d_scores, query_ref[rows, cols], preferred_element_type=jnp.float32)
                * scale
            ).astype(dk_ref.dtype)
            dq_ref[rows, cols] = (
                lax.dot_general(
                    d_scores, key_ref[rows, cols], TN, preferred_element_type=jnp.float32
                )
                * scale
            ).astype(dq_ref.dtype)


def body(queries, keys, values, grad_out, out_weight):
    tok_rows, width = queries.shape
    images, heads = tok_rows // PATCHES, width // HEAD_SIZE
    places, blocks, pieces = gather_both(out_weight, grad_out)
    like = jax.ShapeDtypeStruct(queries.shape, queries.dtype)
    return pl.pallas_call(
        functools.partial(tail_kernel, images, heads),
        out_shape=(like, like, like),
        in_specs=[SMEM] + [ANY] * 12,
        out_specs=(VMEM, VMEM, VMEM),
        scratch_shapes=[
            pltpu.VMEM(queries.shape, jnp.bfloat16),
            pltpu.VMEM(queries.shape, jnp.bfloat16),
            pltpu.VMEM(queries.shape, jnp.bfloat16),
            pltpu.VMEM(blocks.shape, jnp.bfloat16),
            pltpu.VMEM((XLO * QUADS, width, width), jnp.bfloat16),
            pltpu.VMEM((images * heads, PATCHES, PATCHES), jnp.float32),
            pltpu.SemaphoreType.DMA((27,)),
        ],
        name="tail",
        cost_estimate=pl.CostEstimate(
            flops=2 * tok_rows * width * (8 * width + 4 * PATCHES),
            bytes_accessed=2 * (15 * tok_rows * width + 8 * width * width),
            transcendentals=0,
        ),
        compiler_params=pltpu.CompilerParams(vmem_limit_bytes=56 << 20),
    )(places, queries, keys, values, blocks, *pieces)


def solution(mesh):
    placed = (P("dp", "mp"), P("dp", "mp"), P("dp", "mp"), P("dp", "mp"), P("dp", "mp"))
    return jax.shard_map(
        body,
        mesh=mesh,
        in_specs=placed,
        out_specs=(P("dp", "mp"), P("dp", "mp"), P("dp", "mp")),
        check_vma=False,
    )
```

time: 110 us -> 105 us (0.955)
  blocking collectives: 0 us -> 47.7 us
  starting transfers between devices: 66.2 us -> 38.1 us
  waiting for transfers between devices: 25 us -> 4.8 us
  local copies, waits for them, and re-layouts: 8.51 us -> 0.69 us
  Pallas kernels: 8.98 us -> 12.1 us
    all_gather x0 -> x1, blocking collectives: none -> 47.7 us  [far_rows(): return lax.all_gather(weight, 'dp', axis_index_groups=groups)]
    all_to_all x2 -> x1, starting transfers between devices: 37.2 us -> 7.49 us  [gather_both(): lax.all_to_all(arranged_copies(grad, Y * XHI), 'mp', 0, 0, tiled=True)]
    ppermute x1 -> x4, starting transfers between devices: 4.19 us -> 20.8 us  [core_swap(): lax.ppermute(array, 'dp', [(dp_index(x, z, c), dp_index(x, z, 1 - c)) for...]
    ppermute x7 -> x4, starting transfers between devices: 24.8 us -> 9.8 us  [the longest x3 7.89 us: z_shift(): return lax.ppermute(array, 'dp', pairs)]
    ppermute x7 -> x4, waiting for transfers between devices: 18.7 us -> 3.97 us  [the longest x1 3.96 us: x_swap(): lax.ppermute(array, 'dp', [(dp_index(x, z, c), dp_index(1 - x, z, c)) for...]
    unnamed x32 -> x6, local copies, waits for them, and re-layouts: 5.83 us -> 0.01 us
    all_to_all x2 -> x1, waiting for transfers between devices: 4.76 us -> 0.01 us  [gather_both(): lax.all_to_all(arranged_copies(grad, Y * XHI), 'mp', 0, 0, tiled=True)]
    pallas_call x1, Pallas kernels: 6.03 us -> 8.94 us  [body(): pl.pallas_call(functools.partial(tail_kernel, images, heads), out_shape=(...]
  transfers between devices with their start and end apart: 10 -> 9, of which waited for: 8 -> 2; matrix products, arithmetic and copies ran while one was open for 0% -> 1% of each run, Pallas kernels for 3% -> 0%
where the time goes in v3:
time: 105 us; the launch traced here: 104 us
  blocking collectives  47.7 us (45%)
  starting transfers between devices  38.1 us (36%)
  Pallas kernels  12.1 us (12%)
  waiting for transfers between devices  4.8 us (5%)
    all_gather x1, blocking collectives, far_rows(): return lax.all_gather(weight, 'dp', axis_index_groups=groups)  47.7 us
    ppermute x4, starting transfers between devices, core_swap(): lax.ppermute(array, 'dp', [(dp_index(x, z, c), dp_index(x, z, 1 - c)) for...  20.8 us
    pallas_call x1, Pallas kernels, body(): pl.pallas_call(functools.partial(tail_kernel, images, heads), out_shape=(...  8.94 us
    ppermute x3, starting transfers between devices, z_shift(): return lax.ppermute(array, 'dp', pairs)  7.89 us
    all_to_all x1, starting transfers between devices, gather_both(): lax.all_to_all(arranged_copies(grad, Y * XHI), 'mp', 0, 0, tiled=True)  7.49 us
    ppermute x1, waiting for transfers between devices, x_swap(): lax.ppermute(array, 'dp', [(dp_index(x, z, c), dp_index(1 - x, z, c)) for...  3.96 us
    pallas_call x1, Pallas kernels, arranged_copies(): pl.pallas_call(arrange_kernel, out_shape=jax.ShapeDtypeStruct((count, row...  3.17 us
  transfers between devices with their start and end apart: 9, of which 2 were waited for; matrix products, arithmetic and copies ran while one was open for 1% of the time, Pallas kernels for 0%

profile of v3, /device:TPU:1, one launch (start us, length us, event | category | flops | bytes accessed | tf_op | source)
XLA Modules:
  0.0 104.2 jit_solution(10932258091412079329)
XLA Ops:
  0.6 3.2 %arrange.1 = bf16[8,512,384]{2,1,0:T(8,128)(2,1)} custom-call(bf16[512,384]{1,0:T(8,128)(2,1)} %grad_ref.1, bf16[384,384]{1,0:T(8,128)(2,1)} %constant.20.clone.order_ref), custom_call_target="tpu_custom_call" | custom-call | flops 150994944 | bytes 3538944 | tf_op jit(solution)/shard_map/arrange/pallas_call | solution.py:90
  3.8 0.0 copy-start.2
  3.8 7.5 %all-to-all-start = ((bf16[8,512,384]{2,1,0:T(8,128)(2,1)}), bf16[8,512,384]{2,1,0:T(8,128)(2,1)S(1)}, u32[]{:S(2)}, u32[]{:S(2)}) async-start(bf16[8,512,384]{2,1,0:T(8,128)(2,1)} %arrange.1), calls=%async_computation | async-start | bytes 6291456 | tf_op jit(solution)/shard_map/all_to_all | solution.py:113
  11.3 0.0 copy-done.2
  11.3 47.7 %all-gather = bf16[192,384]{1,0:T(8,128)(2,1)S(1)} all-gather(bf16[24,384]{1,0:T(8,128)(2,1)S(1)} %copy-done.2), channel_id=2, replica_groups={{0,64,128,192,256,320,384,448},{8,72,136,200,264,328,392,456},{16,80,14..., dimensions={0}, use_global_device_ids=true | all-gather | bytes 165888 | tf_op jit(solution)/shard_map/all_gather | solution.py:42
  59.0 1.9 %collective-permute-start = (bf16[8,24,384]{2,1,0:T(8,128)(2,1)S(1)}, bf16[8,24,384]{2,1,0:T(8,128)(2,1)S(1)}, u32[]{:S(2)}, u32[]{:S(2)}) collective-permute-start(bf16[8,24,384]{2,1,0:T(8,128)(2,1)S(1)} %bitcast.21), channel_id=1, source_target_pairs={{0,512},{8,520},{16,528},{24,536},{32,544},{40,552},{48,560},{56,5... | collective-permute-start | bytes 442376 | tf_op jit(solution)/shard_map/ppermute | solution.py:53
  60.9 4.0 %collective-permute-done = bf16[8,24,384]{2,1,0:T(8,128)(2,1)S(1)} collective-permute-done((bf16[8,24,384]{2,1,0:T(8,128)(2,1)S(1)}, bf16[8,24,384]{2,1,0:T(8,128)(2,1)S(1)}, u32[]{:S(2)}, u32[]{:S(2)}) %collective-permute-start) | collective-permute-done | bytes 147488 | tf_op jit(solution)/shard_map/ppermute | solution.py:53
  64.9 0.0 copy-start.1
  64.9 0.0 all-to-all-done.blocks
  64.9 0.0 copy-start
  65.0 3.5 %collective-permute-start.3 = (bf16[2,8,24,384]{3,2,1,0:T(8,128)(2,1)S(1)}, bf16[2,8,24,384]{3,2,1,0:T(8,128)(2,1)}, u32[]{:S(2)}, u32[]{:S(2)}) collective-permute-start(bf16[2,8,24,384]{3,2,1,0:T(8,128)(2,1)S(1)} %pad_maximum_fusion), channel_id=1, source_target_pairs={{496,0},{24,8},{0,16},{40,24},{16,32},{56,40},{32,48},{72,56},{48,... | collective-permute-start | bytes 884744 | tf_op jit(solution)/shard_map/ppermute | solution.py:49
  68.5 1.9 %collective-permute-start.2 = (bf16[2,8,24,384]{3,2,1,0:T(8,128)(2,1)S(1)}, bf16[2,8,24,384]{3,2,1,0:T(8,128)(2,1)}, u32[]{:S(2)}, u32[]{:S(2)}) collective-permute-start(bf16[2,8,24,384]{3,2,1,0:T(8,128)(2,1)S(1)} %pad_maximum_fusion), channel_id=1, source_target_pairs={{16,0},{504,8},{32,16},{8,24},{48,32},{24,40},{64,48},{40,56},{80,... | collective-permute-start | bytes 884744 | tf_op jit(solution)/shard_map/ppermute | solution.py:49
  70.4 2.5 %collective-permute-start.1 = (bf16[2,8,24,384]{3,2,1,0:T(8,128)(2,1)S(1)}, bf16[2,8,24,384]{3,2,1,0:T(8,128)(2,1)}, u32[]{:S(2)}, u32[]{:S(2)}) collective-permute-start(bf16[2,8,24,384]{3,2,1,0:T(8,128)(2,1)S(1)} %pad_maximum_fusion), channel_id=1, source_target_pairs={{32,0},{488,8},{48,16},{504,24},{64,32},{8,40},{80,48},{24,56},{96... | collective-permute-start | bytes 884744 | tf_op jit(solution)/shard_map/ppermute | solution.py:49
  72.9 10.1 %collective-permute-start.4 = (bf16[2,8,24,384]{3,2,1,0:T(8,128)(2,1)S(1)}, bf16[2,8,24,384]{3,2,1,0:T(8,128)(2,1)}, u32[]{:S(2)}, u32[]{:S(2)}) collective-permute-start(bf16[2,8,24,384]{3,2,1,0:T(8,128)(2,1)S(1)} %pad_maximum_fusion), channel_id=1, source_target_pairs={{0,8},{8,0},{16,24},{24,16},{32,40},{40,32},{48,56},{56,48},{64,72... | collective-permute-start | bytes 884744 | tf_op jit(solution)/shard_map/ppermute | solution.py:59
  82.9 0.0 collective-permute-done.3
  83.0 6.4 %collective-permute-start.7 = (bf16[2,8,24,384]{3,2,1,0:T(8,128)(2,1)}, bf16[2,8,24,384]{3,2,1,0:T(8,128)(2,1)}, u32[]{:S(2)}, u32[]{:S(2)}) collective-permute-start(bf16[2,8,24,384]{3,2,1,0:T(8,128)(2,1)} %collective-permute-done.3), channel_id=1, source_target_pairs={{0,8},{8,0},{16,24},{24,16},{32,40},{40,32},{48,56},{56,48},{64,72... | collective-permute-start | bytes 884744 | tf_op jit(solution)/shard_map/ppermute | solution.py:59
  89.3 0.0 collective-permute-done.2
  89.3 1.9 %collective-permute-start.6 = (bf16[2,8,24,384]{3,2,1,0:T(8,128)(2,1)}, bf16[2,8,24,384]{3,2,1,0:T(8,128)(2,1)}, u32[]{:S(2)}, u32[]{:S(2)}) collective-permute-start(bf16[2,8,24,384]{3,2,1,0:T(8,128)(2,1)} %collective-permute-done.2), channel_id=1, source_target_pairs={{0,8},{8,0},{16,24},{24,16},{32,40},{40,32},{48,56},{56,48},{64,72... | collective-permute-start | bytes 884744 | tf_op jit(solution)/shard_map/ppermute | solution.py:59
  91.3 0.0 collective-permute-done.1
  91.3 2.4 %collective-permute-start.5 = (bf16[2,8,24,384]{3,2,1,0:T(8,128)(2,1)}, bf16[2,8,24,384]{3,2,1,0:T(8,128)(2,1)}, u32[]{:S(2)}, u32[]{:S(2)}) collective-permute-start(bf16[2,8,24,384]{3,2,1,0:T(8,128)(2,1)} %collective-permute-done.1), channel_id=1, source_target_pairs={{0,8},{8,0},{16,24},{24,16},{32,40},{40,32},{48,56},{56,48},{64,72... | collective-permute-start | bytes 884744 | tf_op jit(solution)/shard_map/ppermute | solution.py:59
  93.7 0.7 stack.49.place_ref
  94.4 0.0 collective-permute-done.4
  94.4 0.0 collective-permute-done.7
  94.4 0.0 collective-permute-done.6
  94.4 0.8 collective-permute-done.5
  95.2 0.0 copy-done.1
  95.2 0.0 copy-done
  95.2 8.9 %tail.1 = (bf16[512,384]{1,0:T(8,128)(2,1)}, bf16[512,384]{1,0:T(8,128)(2,1)}, bf16[512,384]{1,0:T(8,128)(2,1)}) custom-call(s32[10]{0:T(128)} %stack.49.place_ref, bf16[512,384]{1,0:T(8,128)(2,1)} %queries.1, bf16[512,384]{1,0:T(8,128)(2,1)} %keys.1, bf16[512,384]{1,0:T(8,128)(2,1)} %values.1, bf16[8,512,384]{2,1,0:T(8,128)(2,1)} %copy-done, ...), custom_call_target="tpu_custom_call" | custom-call | flops 1610612736 | bytes 8257536 | tf_op jit(solution)/shard_map/tail/pallas_call | solution.py:212
  (1 shorter events, 0.0 us)
Async XLA Ops:
  3.8 7.5 %copy-start.2 = (bf16[24,384]{1,0:T(8,128)(2,1)S(1)}, bf16[24,384]{1,0:T(8,128)(2,1)}, u32[]{:S(2)}) copy-start(bf16[24,384]{1,0:T(8,128)(2,1)} %param.10) | copy-start | bytes 55300
  3.8 61.1 %all-to-all-start = ((bf16[8,512,384]{2,1,0:T(8,128)(2,1)}), bf16[8,512,384]{2,1,0:T(8,128)(2,1)S(1)}, u32[]{:S(2)}, u32[]{:S(2)}) async-start(bf16[8,512,384]{2,1,0:T(8,128)(2,1)} %arrange.1), calls=%async_computation | async-start | bytes 6291456 | tf_op jit(solution)/shard_map/all_to_all | solution.py:113
  59.0 5.9 %collective-permute-start = (bf16[8,24,384]{2,1,0:T(8,128)(2,1)S(1)}, bf16[8,24,384]{2,1,0:T(8,128)(2,1)S(1)}, u32[]{:S(2)}, u32[]{:S(2)}) collective-permute-start(bf16[8,24,384]{2,1,0:T(8,128)(2,1)S(1)} %bitcast.21), channel_id=1, source_target_pairs={{0,512},{8,520},{16,528},{24,536},{32,544},{40,552},{48,560},{56,5... | collective-permute-start | bytes 442376 | tf_op jit(solution)/shard_map/ppermute | solution.py:53
  64.9 30.3 %copy-start.1 = (bf16[2,8,24,384]{3,2,1,0:T(8,128)(2,1)}, bf16[2,8,24,384]{3,2,1,0:T(8,128)(2,1)S(1)}, u32[]{:S(2)}) copy-start(bf16[2,8,24,384]{3,2,1,0:T(8,128)(2,1)S(1)} %pad_maximum_fusion) | copy-start | bytes 884740
  64.9 30.3 %copy-start = (bf16[8,512,384]{2,1,0:T(8,128)(2,1)}, bf16[8,512,384]{2,1,0:T(8,128)(2,1)S(1)}, u32[]{:S(2)}) copy-start(bf16[8,512,384]{2,1,0:T(8,128)(2,1)S(1)} %all-to-all-done.blocks) | copy-start | bytes 9437188
  65.0 18.0 %collective-permute-start.3 = (bf16[2,8,24,384]{3,2,1,0:T(8,128)(2,1)S(1)}, bf16[2,8,24,384]{3,2,1,0:T(8,128)(2,1)}, u32[]{:S(2)}, u32[]{:S(2)}) collective-permute-start(bf16[2,8,24,384]{3,2,1,0:T(8,128)(2,1)S(1)} %pad_maximum_fusion), channel_id=1, source_target_pairs={{496,0},{24,8},{0,16},{40,24},{16,32},{56,40},{32,48},{72,56},{48,... | collective-permute-start | bytes 884744 | tf_op jit(solution)/shard_map/ppermute | solution.py:49
  68.5 20.9 %collective-permute-start.2 = (bf16[2,8,24,384]{3,2,1,0:T(8,128)(2,1)S(1)}, bf16[2,8,24,384]{3,2,1,0:T(8,128)(2,1)}, u32[]{:S(2)}, u32[]{:S(2)}) collective-permute-start(bf16[2,8,24,384]{3,2,1,0:T(8,128)(2,1)S(1)} %pad_maximum_fusion), channel_id=1, source_target_pairs={{16,0},{504,8},{32,16},{8,24},{48,32},{24,40},{64,48},{40,56},{80,... | collective-permute-start | bytes 884744 | tf_op jit(solution)/shard_map/ppermute | solution.py:49
  70.4 20.9 %collective-permute-start.1 = (bf16[2,8,24,384]{3,2,1,0:T(8,128)(2,1)S(1)}, bf16[2,8,24,384]{3,2,1,0:T(8,128)(2,1)}, u32[]{:S(2)}, u32[]{:S(2)}) collective-permute-start(bf16[2,8,24,384]{3,2,1,0:T(8,128)(2,1)S(1)} %pad_maximum_fusion), channel_id=1, source_target_pairs={{32,0},{488,8},{48,16},{504,24},{64,32},{8,40},{80,48},{24,56},{96... | collective-permute-start | bytes 884744 | tf_op jit(solution)/shard_map/ppermute | solution.py:49
  72.9 21.5 %collective-permute-start.4 = (bf16[2,8,24,384]{3,2,1,0:T(8,128)(2,1)S(1)}, bf16[2,8,24,384]{3,2,1,0:T(8,128)(2,1)}, u32[]{:S(2)}, u32[]{:S(2)}) collective-permute-start(bf16[2,8,24,384]{3,2,1,0:T(8,128)(2,1)S(1)} %pad_maximum_fusion), channel_id=1, source_target_pairs={{0,8},{8,0},{16,24},{24,16},{32,40},{40,32},{48,56},{56,48},{64,72... | collective-permute-start | bytes 884744 | tf_op jit(solution)/shard_map/ppermute | solution.py:59
  83.0 11.4 %collective-permute-start.7 = (bf16[2,8,24,384]{3,2,1,0:T(8,128)(2,1)}, bf16[2,8,24,384]{3,2,1,0:T(8,128)(2,1)}, u32[]{:S(2)}, u32[]{:S(2)}) collective-permute-start(bf16[2,8,24,384]{3,2,1,0:T(8,128)(2,1)} %collective-permute-done.3), channel_id=1, source_target_pairs={{0,8},{8,0},{16,24},{24,16},{32,40},{40,32},{48,56},{56,48},{64,72... | collective-permute-start | bytes 884744 | tf_op jit(solution)/shard_map/ppermute | solution.py:59
  89.3 5.1 %collective-permute-start.6 = (bf16[2,8,24,384]{3,2,1,0:T(8,128)(2,1)}, bf16[2,8,24,384]{3,2,1,0:T(8,128)(2,1)}, u32[]{:S(2)}, u32[]{:S(2)}) collective-permute-start(bf16[2,8,24,384]{3,2,1,0:T(8,128)(2,1)} %collective-permute-done.2), channel_id=1, source_target_pairs={{0,8},{8,0},{16,24},{24,16},{32,40},{40,32},{48,56},{56,48},{64,72... | collective-permute-start | bytes 884744 | tf_op jit(solution)/shard_map/ppermute | solution.py:59
  91.3 3.9 %collective-permute-start.5 = (bf16[2,8,24,384]{3,2,1,0:T(8,128)(2,1)}, bf16[2,8,24,384]{3,2,1,0:T(8,128)(2,1)}, u32[]{:S(2)}, u32[]{:S(2)}) collective-permute-start(bf16[2,8,24,384]{3,2,1,0:T(8,128)(2,1)} %collective-permute-done.1), channel_id=1, source_target_pairs={{0,8},{8,0},{16,24},{24,16},{32,40},{40,32},{48,56},{56,48},{64,72... | collective-permute-start | bytes 884744 | tf_op jit(solution)/shard_map/ppermute | solution.py:59

commit v4 on v3

--- a/solution.py
+++ b/solution.py
@@ -105,7 +105,7 @@
     )(grad, arrange_columns(width))
 
 
-STEPS = (0, 2, 1, -1)
+STEPS = (0, -1, 1, 2)
 
 
 def gather_both(weight, grad):
@@ -119,28 +119,24 @@
     pieces = [
         piece.reshape(XLO, QUADS, HALVES * rows, width) for piece in pieces
     ]
-    here = lax.axis_index("dp")
-    core, z, x = here & 1, (here >> 1) & (Z - 1), here >> 6
-    residues = [
-        (z + (1 - 2 * c) * step) & (STRIDE - 1) for c in (core, 1 - core) for step in STEPS
-    ]
-    places = jnp.stack(residues + [core, x]).astype(jnp.int32)
-    return places, blocks, pieces
-
-
-def tail_kernel(images, heads, place_ref, queries, keys, values, blocks, *rest):
+    return blocks, pieces
+
+
+def tail_kernel(images, heads, here_ref, queries, keys, values, blocks, *rest):
     pieces, (dq_ref, dk_ref, dv_ref), scratch = rest[:8], rest[8:11], rest[11:]
     query_ref, key_ref, value_ref, blocks_ref, weight_ref, probs_ref, sems = scratch
     scale = 1.0 / math.sqrt(HEAD_SIZE)
     group = pieces[0].shape[2]
     count = XLO * QUADS
-    core, here = place_ref[8], place_ref[9]
+    here = here_ref[0]
+    core, z, here_x = here & 1, (here >> 1) & (Z - 1), here >> 6
     copies = [(queries, query_ref), (keys, key_ref)]
     for p, piece in enumerate(pieces):
         c = core if p < 4 else 1 - core
-        start = pl.multiple_of((c * STRIDE + place_ref[p]) * group, 16)
+        residue = (z + (1 - 2 * c) * STEPS[p % 4]) & (STRIDE - 1)
+        start = pl.multiple_of((c * STRIDE + residue) * group, 16)
         for away in range(XLO):
-            x = here if away == 0 else 1 - here
+            x = here_x if away == 0 else 1 - here_x
             there = weight_ref.at[pl.ds(x * QUADS, QUADS), pl.ds(start, group)]
             copies.append((piece.at[away], there))
     copies += [(blocks.at[j], blocks_ref.at[j]) for j in range(count)]
@@ -207,7 +203,8 @@
 def body(queries, keys, values, grad_out, out_weight):
     tok_rows, width = queries.shape
     images, heads = tok_rows // PATCHES, width // HEAD_SIZE
-    places, blocks, pieces = gather_both(out_weight, grad_out)
+    blocks, pieces = gather_both(out_weight, grad_out)
+    here = lax.axis_index("dp").astype(jnp.int32).reshape(1)
     like = jax.ShapeDtypeStruct(queries.shape, queries.dtype)
     return pl.pallas_call(
         functools.partial(tail_kernel, images, heads),
@@ -230,7 +227,7 @@
             transcendentals=0,
         ),
         compiler_params=pltpu.CompilerParams(vmem_limit_bytes=56 << 20),
-    )(places, queries, keys, values, blocks, *pieces)
+    )(here, queries, keys, values, blocks, *pieces)
 
 
 def solution(mesh):

time: 105 us -> 102 us (0.971)
  starting transfers between devices: 38.1 us -> 36.3 us
    ppermute x4, starting transfers between devices: 20.8 us -> 17.8 us  [core_swap(): lax.ppermute(array, 'dp', [(dp_index(x, z, c), dp_index(x, z, 1 - c)) for...]
    ppermute x3, starting transfers between devices: 7.89 us -> 9.1 us  [z_shift(): return lax.ppermute(array, 'dp', pairs)]
  transfers between devices with their start and end apart: 9 -> 9, of which waited for: 2 -> 2; matrix products, arithmetic and copies ran while one was open for 1% -> 0% of each run, Pallas kernels for 0% -> 0%
where the time goes in v4:
time: 102 us
  blocking collectives  47.7 us (47%)
  starting transfers between devices  36.3 us (36%)
  Pallas kernels  11.5 us (11%)
  waiting for transfers between devices  5.65 us (6%)
    all_gather x1, blocking collectives, far_rows(): return lax.all_gather(weight, 'dp', axis_index_groups=groups)  47.7 us
    ppermute x4, starting transfers between devices, core_swap(): lax.ppermute(array, 'dp', [(dp_index(x, z, c), dp_index(x, z, 1 - c)) for...  17.8 us
    ppermute x3, starting transfers between devices, z_shift(): return lax.ppermute(array, 'dp', pairs)  9.1 us
    pallas_call x1, Pallas kernels, body(): pl.pallas_call(functools.partial(tail_kernel, images, heads), out_shape=(...  8.29 us
    all_to_all x1, starting transfers between devices, gather_both(): lax.all_to_all(arranged_copies(grad, Y * XHI), 'mp', 0, 0, tiled=True)  7.49 us
    ppermute x1, waiting for transfers between devices, x_swap(): lax.ppermute(array, 'dp', [(dp_index(x, z, c), dp_index(1 - x, z, c)) for...  3.96 us
    pallas_call x1, Pallas kernels, arranged_copies(): pl.pallas_call(arrange_kernel, out_shape=jax.ShapeDtypeStruct((count, row...  3.17 us
  transfers between devices with their start and end apart: 9, of which 2 were waited for; matrix products, arithmetic and copies ran while one was open for 0% of the time, Pallas kernels for 0%

profile of v4, /device:TPU:1, one launch (start us, length us, event | category | flops | bytes accessed | tf_op | source)
XLA Modules:
  0.0 101.9 jit_solution(12221191982715804697)
XLA Ops:
  0.6 3.2 %arrange.1 = bf16[8,512,384]{2,1,0:T(8,128)(2,1)} custom-call(bf16[512,384]{1,0:T(8,128)(2,1)} %grad_ref.1, bf16[384,384]{1,0:T(8,128)(2,1)} %constant.8.clone.order_ref), custom_call_target="tpu_custom_call" | custom-call | flops 150994944 | bytes 3538944 | tf_op jit(solution)/shard_map/arrange/pallas_call | solution.py:90
  3.8 0.0 copy-start.2
  3.8 7.5 %all-to-all-start = ((bf16[8,512,384]{2,1,0:T(8,128)(2,1)}), bf16[8,512,384]{2,1,0:T(8,128)(2,1)S(1)}, u32[]{:S(2)}, u32[]{:S(2)}) async-start(bf16[8,512,384]{2,1,0:T(8,128)(2,1)} %arrange.1), calls=%async_computation | async-start | bytes 6291456 | tf_op jit(solution)/shard_map/all_to_all | solution.py:113
  11.3 0.0 copy-done.2
  11.3 47.7 %all-gather = bf16[192,384]{1,0:T(8,128)(2,1)S(1)} all-gather(bf16[24,384]{1,0:T(8,128)(2,1)S(1)} %copy-done.2), channel_id=2, replica_groups={{0,64,128,192,256,320,384,448},{8,72,136,200,264,328,392,456},{16,80,14..., dimensions={0}, use_global_device_ids=true | all-gather | bytes 165888 | tf_op jit(solution)/shard_map/all_gather | solution.py:42
  59.0 1.9 %collective-permute-start = (bf16[8,24,384]{2,1,0:T(8,128)(2,1)S(1)}, bf16[8,24,384]{2,1,0:T(8,128)(2,1)S(1)}, u32[]{:S(2)}, u32[]{:S(2)}) collective-permute-start(bf16[8,24,384]{2,1,0:T(8,128)(2,1)S(1)} %bitcast.13), channel_id=1, source_target_pairs={{0,512},{8,520},{16,528},{24,536},{32,544},{40,552},{48,560},{56,5... | collective-permute-start | bytes 442376 | tf_op jit(solution)/shard_map/ppermute | solution.py:53
  60.9 4.0 %collective-permute-done = bf16[8,24,384]{2,1,0:T(8,128)(2,1)S(1)} collective-permute-done((bf16[8,24,384]{2,1,0:T(8,128)(2,1)S(1)}, bf16[8,24,384]{2,1,0:T(8,128)(2,1)S(1)}, u32[]{:S(2)}, u32[]{:S(2)}) %collective-permute-start) | collective-permute-done | bytes 147488 | tf_op jit(solution)/shard_map/ppermute | solution.py:53
  64.9 0.0 copy-start.1
  64.9 0.0 all-to-all-done.blocks
  64.9 0.0 copy-start
  65.0 2.6 %collective-permute-start.3 = (bf16[2,8,24,384]{3,2,1,0:T(8,128)(2,1)S(1)}, bf16[2,8,24,384]{3,2,1,0:T(8,128)(2,1)}, u32[]{:S(2)}, u32[]{:S(2)}) collective-permute-start(bf16[2,8,24,384]{3,2,1,0:T(8,128)(2,1)S(1)} %pad_maximum_fusion), channel_id=1, source_target_pairs={{32,0},{488,8},{48,16},{504,24},{64,32},{8,40},{80,48},{24,56},{96... | collective-permute-start | bytes 884744 | tf_op jit(solution)/shard_map/ppermute | solution.py:49
  67.6 2.6 %collective-permute-start.2 = (bf16[2,8,24,384]{3,2,1,0:T(8,128)(2,1)S(1)}, bf16[2,8,24,384]{3,2,1,0:T(8,128)(2,1)}, u32[]{:S(2)}, u32[]{:S(2)}) collective-permute-start(bf16[2,8,24,384]{3,2,1,0:T(8,128)(2,1)S(1)} %pad_maximum_fusion), channel_id=1, source_target_pairs={{16,0},{504,8},{32,16},{8,24},{48,32},{24,40},{64,48},{40,56},{80,... | collective-permute-start | bytes 884744 | tf_op jit(solution)/shard_map/ppermute | solution.py:49
  70.1 3.9 %collective-permute-start.1 = (bf16[2,8,24,384]{3,2,1,0:T(8,128)(2,1)S(1)}, bf16[2,8,24,384]{3,2,1,0:T(8,128)(2,1)}, u32[]{:S(2)}, u32[]{:S(2)}) collective-permute-start(bf16[2,8,24,384]{3,2,1,0:T(8,128)(2,1)S(1)} %pad_maximum_fusion), channel_id=1, source_target_pairs={{496,0},{24,8},{0,16},{40,24},{16,32},{56,40},{32,48},{72,56},{48,... | collective-permute-start | bytes 884744 | tf_op jit(solution)/shard_map/ppermute | solution.py:49
  74.1 8.9 %collective-permute-start.4 = (bf16[2,8,24,384]{3,2,1,0:T(8,128)(2,1)S(1)}, bf16[2,8,24,384]{3,2,1,0:T(8,128)(2,1)}, u32[]{:S(2)}, u32[]{:S(2)}) collective-permute-start(bf16[2,8,24,384]{3,2,1,0:T(8,128)(2,1)S(1)} %pad_maximum_fusion), channel_id=1, source_target_pairs={{0,8},{8,0},{16,24},{24,16},{32,40},{40,32},{48,56},{56,48},{64,72... | collective-permute-start | bytes 884744 | tf_op jit(solution)/shard_map/ppermute | solution.py:59
  82.9 0.0 collective-permute-done.3
  83.0 4.6 %collective-permute-start.7 = (bf16[2,8,24,384]{3,2,1,0:T(8,128)(2,1)}, bf16[2,8,24,384]{3,2,1,0:T(8,128)(2,1)}, u32[]{:S(2)}, u32[]{:S(2)}) collective-permute-start(bf16[2,8,24,384]{3,2,1,0:T(8,128)(2,1)} %collective-permute-done.3), channel_id=1, source_target_pairs={{0,8},{8,0},{16,24},{24,16},{32,40},{40,32},{48,56},{56,48},{64,72... | collective-permute-start | bytes 884744 | tf_op jit(solution)/shard_map/ppermute | solution.py:59
  87.5 0.0 collective-permute-done.2
  87.6 2.2 %collective-permute-start.6 = (bf16[2,8,24,384]{3,2,1,0:T(8,128)(2,1)}, bf16[2,8,24,384]{3,2,1,0:T(8,128)(2,1)}, u32[]{:S(2)}, u32[]{:S(2)}) collective-permute-start(bf16[2,8,24,384]{3,2,1,0:T(8,128)(2,1)} %collective-permute-done.2), channel_id=1, source_target_pairs={{0,8},{8,0},{16,24},{24,16},{32,40},{40,32},{48,56},{56,48},{64,72... | collective-permute-start | bytes 884744 | tf_op jit(solution)/shard_map/ppermute | solution.py:59
  89.8 0.0 collective-permute-done.1
  89.8 2.1 %collective-permute-start.5 = (bf16[2,8,24,384]{3,2,1,0:T(8,128)(2,1)}, bf16[2,8,24,384]{3,2,1,0:T(8,128)(2,1)}, u32[]{:S(2)}, u32[]{:S(2)}) collective-permute-start(bf16[2,8,24,384]{3,2,1,0:T(8,128)(2,1)} %collective-permute-done.1), channel_id=1, source_target_pairs={{0,8},{8,0},{16,24},{24,16},{32,40},{40,32},{48,56},{56,48},{64,72... | collective-permute-start | bytes 884744 | tf_op jit(solution)/shard_map/ppermute | solution.py:59
  91.9 0.0 collective-permute-done.4
  91.9 0.0 collective-permute-done.7
  91.9 0.0 collective-permute-done.6
  91.9 1.7 %collective-permute-done.5 = bf16[2,8,24,384]{3,2,1,0:T(8,128)(2,1)} collective-permute-done((bf16[2,8,24,384]{3,2,1,0:T(8,128)(2,1)}, bf16[2,8,24,384]{3,2,1,0:T(8,128)(2,1)}, u32[]{:S(2)}, u32[]{:S(2)}) %collective-permute-start.5) | collective-permute-done | bytes 294944 | tf_op jit(solution)/shard_map/ppermute | solution.py:59
  93.6 0.0 copy-done.1
  93.6 0.0 copy-done
  93.6 8.3 %tail.1 = (bf16[512,384]{1,0:T(8,128)(2,1)}, bf16[512,384]{1,0:T(8,128)(2,1)}, bf16[512,384]{1,0:T(8,128)(2,1)}) custom-call(s32[1]{0:T(128)} %bitcast.here_ref, bf16[512,384]{1,0:T(8,128)(2,1)} %queries.1, bf16[512,384]{1,0:T(8,128)(2,1)} %keys.1, bf16[512,384]{1,0:T(8,128)(2,1)} %values.1, bf16[8,512,384]{2,1,0:T(8,128)(2,1)} %copy-done, ...), custom_call_target="tpu_custom_call" | custom-call | flops 1610612736 | bytes 8257536 | tf_op jit(solution)/shard_map/tail/pallas_call | solution.py:209
  (1 shorter events, 0.0 us)
Async XLA Ops:
  3.8 7.5 %copy-start.2 = (bf16[24,384]{1,0:T(8,128)(2,1)S(1)}, bf16[24,384]{1,0:T(8,128)(2,1)}, u32[]{:S(2)}) copy-start(bf16[24,384]{1,0:T(8,128)(2,1)} %param.10) | copy-start | bytes 55300
  3.8 61.1 %all-to-all-start = ((bf16[8,512,384]{2,1,0:T(8,128)(2,1)}), bf16[8,512,384]{2,1,0:T(8,128)(2,1)S(1)}, u32[]{:S(2)}, u32[]{:S(2)}) async-start(bf16[8,512,384]{2,1,0:T(8,128)(2,1)} %arrange.1), calls=%async_computation | async-start | bytes 6291456 | tf_op jit(solution)/shard_map/all_to_all | solution.py:113
  59.0 5.9 %collective-permute-start = (bf16[8,24,384]{2,1,0:T(8,128)(2,1)S(1)}, bf16[8,24,384]{2,1,0:T(8,128)(2,1)S(1)}, u32[]{:S(2)}, u32[]{:S(2)}) collective-permute-start(bf16[8,24,384]{2,1,0:T(8,128)(2,1)S(1)} %bitcast.13), channel_id=1, source_target_pairs={{0,512},{8,520},{16,528},{24,536},{32,544},{40,552},{48,560},{56,5... | collective-permute-start | bytes 442376 | tf_op jit(solution)/shard_map/ppermute | solution.py:53
  64.9 28.7 %copy-start.1 = (bf16[2,8,24,384]{3,2,1,0:T(8,128)(2,1)}, bf16[2,8,24,384]{3,2,1,0:T(8,128)(2,1)S(1)}, u32[]{:S(2)}) copy-start(bf16[2,8,24,384]{3,2,1,0:T(8,128)(2,1)S(1)} %pad_maximum_fusion) | copy-start | bytes 884740
  64.9 28.7 %copy-start = (bf16[8,512,384]{2,1,0:T(8,128)(2,1)}, bf16[8,512,384]{2,1,0:T(8,128)(2,1)S(1)}, u32[]{:S(2)}) copy-start(bf16[8,512,384]{2,1,0:T(8,128)(2,1)S(1)} %all-to-all-done.blocks) | copy-start | bytes 9437188
  65.0 18.0 %collective-permute-start.3 = (bf16[2,8,24,384]{3,2,1,0:T(8,128)(2,1)S(1)}, bf16[2,8,24,384]{3,2,1,0:T(8,128)(2,1)}, u32[]{:S(2)}, u32[]{:S(2)}) collective-permute-start(bf16[2,8,24,384]{3,2,1,0:T(8,128)(2,1)S(1)} %pad_maximum_fusion), channel_id=1, source_target_pairs={{32,0},{488,8},{48,16},{504,24},{64,32},{8,40},{80,48},{24,56},{96... | collective-permute-start | bytes 884744 | tf_op jit(solution)/shard_map/ppermute | solution.py:49
  67.6 20.0 %collective-permute-start.2 = (bf16[2,8,24,384]{3,2,1,0:T(8,128)(2,1)S(1)}, bf16[2,8,24,384]{3,2,1,0:T(8,128)(2,1)}, u32[]{:S(2)}, u32[]{:S(2)}) collective-permute-start(bf16[2,8,24,384]{3,2,1,0:T(8,128)(2,1)S(1)} %pad_maximum_fusion), channel_id=1, source_target_pairs={{16,0},{504,8},{32,16},{8,24},{48,32},{24,40},{64,48},{40,56},{80,... | collective-permute-start | bytes 884744 | tf_op jit(solution)/shard_map/ppermute | solution.py:49
  70.1 19.7 %collective-permute-start.1 = (bf16[2,8,24,384]{3,2,1,0:T(8,128)(2,1)S(1)}, bf16[2,8,24,384]{3,2,1,0:T(8,128)(2,1)}, u32[]{:S(2)}, u32[]{:S(2)}) collective-permute-start(bf16[2,8,24,384]{3,2,1,0:T(8,128)(2,1)S(1)} %pad_maximum_fusion), channel_id=1, source_target_pairs={{496,0},{24,8},{0,16},{40,24},{16,32},{56,40},{32,48},{72,56},{48,... | collective-permute-start | bytes 884744 | tf_op jit(solution)/shard_map/ppermute | solution.py:49
  74.1 17.8 %collective-permute-start.4 = (bf16[2,8,24,384]{3,2,1,0:T(8,128)(2,1)S(1)}, bf16[2,8,24,384]{3,2,1,0:T(8,128)(2,1)}, u32[]{:S(2)}, u32[]{:S(2)}) collective-permute-start(bf16[2,8,24,384]{3,2,1,0:T(8,128)(2,1)S(1)} %pad_maximum_fusion), channel_id=1, source_target_pairs={{0,8},{8,0},{16,24},{24,16},{32,40},{40,32},{48,56},{56,48},{64,72... | collective-permute-start | bytes 884744 | tf_op jit(solution)/shard_map/ppermute | solution.py:59
  83.0 9.0 %collective-permute-start.7 = (bf16[2,8,24,384]{3,2,1,0:T(8,128)(2,1)}, bf16[2,8,24,384]{3,2,1,0:T(8,128)(2,1)}, u32[]{:S(2)}, u32[]{:S(2)}) collective-permute-start(bf16[2,8,24,384]{3,2,1,0:T(8,128)(2,1)} %collective-permute-done.3), channel_id=1, source_target_pairs={{0,8},{8,0},{16,24},{24,16},{32,40},{40,32},{48,56},{56,48},{64,72... | collective-permute-start | bytes 884744 | tf_op jit(solution)/shard_map/ppermute | solution.py:59
  87.6 4.4 %collective-permute-start.6 = (bf16[2,8,24,384]{3,2,1,0:T(8,128)(2,1)}, bf16[2,8,24,384]{3,2,1,0:T(8,128)(2,1)}, u32[]{:S(2)}, u32[]{:S(2)}) collective-permute-start(bf16[2,8,24,384]{3,2,1,0:T(8,128)(2,1)} %collective-permute-done.2), channel_id=1, source_target_pairs={{0,8},{8,0},{16,24},{24,16},{32,40},{40,32},{48,56},{56,48},{64,72... | collective-permute-start | bytes 884744 | tf_op jit(solution)/shard_map/ppermute | solution.py:59
  89.8 3.8 %collective-permute-start.5 = (bf16[2,8,24,384]{3,2,1,0:T(8,128)(2,1)}, bf16[2,8,24,384]{3,2,1,0:T(8,128)(2,1)}, u32[]{:S(2)}, u32[]{:S(2)}) collective-permute-start(bf16[2,8,24,384]{3,2,1,0:T(8,128)(2,1)} %collective-permute-done.1), channel_id=1, source_target_pairs={{0,8},{8,0},{16,24},{24,16},{32,40},{40,32},{48,56},{56,48},{64,72... | collective-permute-start | bytes 884744 | tf_op jit(solution)/shard_map/ppermute | solution.py:59

commit v5 on v4

--- a/solution.py
+++ b/solution.py
@@ -73,14 +73,16 @@
 
 
 def arrange_kernel(grad_ref, order_ref, out_ref, held, sems):
-    held[...] = jnp.dot(
-        grad_ref[...], order_ref[...], preferred_element_type=jnp.float32
-    ).astype(held.dtype)
-    copies = [
-        pltpu.make_async_copy(held, out_ref.at[p], sems.at[p]) for p in range(out_ref.shape[0])
-    ]
-    for copy in copies:
-        copy.start()
+    copies = []
+    for half in range(2):
+        rows = pl.ds(half * PATCHES, PATCHES)
+        held[rows, :] = jnp.dot(
+            grad_ref[rows, :], order_ref[...], preferred_element_type=jnp.float32
+        ).astype(held.dtype)
+        for p in range(out_ref.shape[0]):
+            copy = pltpu.make_async_copy(held.at[rows], out_ref.at[p, rows], sems.at[half, p])
+            copy.start()
+            copies.append(copy)
     for copy in copies:
         copy.wait()
 
@@ -94,7 +96,7 @@
         out_specs=ANY,
         scratch_shapes=[
             pltpu.VMEM((rows, width), grad.dtype),
-            pltpu.SemaphoreType.DMA((count,)),
+            pltpu.SemaphoreType.DMA((2, count)),
         ],
         name="arrange",
         cost_estimate=pl.CostEstimate(
@@ -123,8 +125,9 @@
 
 
 def tail_kernel(images, heads, here_ref, queries, keys, values, blocks, *rest):
-    pieces, (dq_ref, dk_ref, dv_ref), scratch = rest[:8], rest[8:11], rest[11:]
-    query_ref, key_ref, value_ref, blocks_ref, weight_ref, probs_ref, sems = scratch
+    pieces, outs, scratch = rest[:8], rest[8:11], rest[11:]
+    query_ref, key_ref, value_ref, blocks_ref, weight_ref, probs_ref = scratch[:6]
+    dq_ref, dk_ref, dv_ref, sems, out_sems = scratch[6:]
     scale = 1.0 / math.sqrt(HEAD_SIZE)
     group = pieces[0].shape[2]
     count = XLO * QUADS
@@ -163,6 +166,7 @@
             probs_ref[image * heads + head] = exped / jnp.sum(exped, axis=0, keepdims=True)
     for copy in copies[2:18]:
         copy.wait()
+    writes = []
     for image in range(images):
         rows = pl.ds(image * PATCHES, PATCHES)
         total = None
@@ -198,6 +202,14 @@
                 )
                 * scale
             ).astype(dq_ref.dtype)
+        for i, stage in enumerate((dq_ref, dk_ref, dv_ref)):
+            write = pltpu.make_async_copy(
+                stage.at[rows], outs[i].at[rows], out_sems.at[image, i]
+            )
+            write.start()
+            writes.append(write)
+    for write in writes:
+        write.wait()
 
 
 def body(queries, keys, values, grad_out, out_weight):
@@ -210,7 +222,7 @@
         functools.partial(tail_kernel, images, heads),
         out_shape=(like, like, like),
         in_specs=[SMEM] + [ANY] * 12,
-        out_specs=(VMEM, VMEM, VMEM),
+        out_specs=(ANY, ANY, ANY),
         scratch_shapes=[
             pltpu.VMEM(queries.shape, jnp.bfloat16),
             pltpu.VMEM(queries.shape, jnp.bfloat16),
@@ -218,7 +230,11 @@
             pltpu.VMEM(blocks.shape, jnp.bfloat16),
             pltpu.VMEM((XLO * QUADS, width, width), jnp.bfloat16),
             pltpu.VMEM((images * heads, PATCHES, PATCHES), jnp.float32),
+            pltpu.VMEM(queries.shape, jnp.bfloat16),
+            pltpu.VMEM(queries.shape, jnp.bfloat16),
+            pltpu.VMEM(queries.shape, jnp.bfloat16),
             pltpu.SemaphoreType.DMA((27,)),
+            pltpu.SemaphoreType.DMA((images, 3)),
         ],
         name="tail",
         cost_estimate=pl.CostEstimate(

time: 102 us -> 102 us (level)
  no operation moved by 1% of the time
where the time goes in v5:
time: 102 us
  blocking collectives  47.7 us (47%)
  starting transfers between devices  36.3 us (36%)
  Pallas kernels  11.3 us (11%)
  waiting for transfers between devices  5.66 us (6%)
    all_gather x1, blocking collectives, far_rows(): return lax.all_gather(weight, 'dp', axis_index_groups=groups)  47.7 us
    ppermute x4, starting transfers between devices, core_swap(): lax.ppermute(array, 'dp', [(dp_index(x, z, c), dp_index(x, z, 1 - c)) for...  17.8 us
    ppermute x3, starting transfers between devices, z_shift(): return lax.ppermute(array, 'dp', pairs)  9.1 us
    pallas_call x1, Pallas kernels, body(): pl.pallas_call(functools.partial(tail_kernel, images, heads), out_shape=(...  8.18 us
    all_to_all x1, starting transfers between devices, gather_both(): lax.all_to_all(arranged_copies(grad, Y * XHI), 'mp', 0, 0, tiled=True)  7.49 us
    ppermute x1, waiting for transfers between devices, x_swap(): lax.ppermute(array, 'dp', [(dp_index(x, z, c), dp_index(1 - x, z, c)) for...  3.96 us
    pallas_call x1, Pallas kernels, arranged_copies(): pl.pallas_call(arrange_kernel, out_shape=jax.ShapeDtypeStruct((count, row...  3.14 us
  transfers between devices with their start and end apart: 9, of which 2 were waited for; matrix products, arithmetic and copies ran while one was open for 0% of the time, Pallas kernels for 0%

profile of v5, /device:TPU:1, one launch (start us, length us, event | category | flops | bytes accessed | tf_op | source)
XLA Modules:
  0.0 101.8 jit_solution(11461592595053036454)
XLA Ops:
  0.6 3.1 %arrange.1 = bf16[8,512,384]{2,1,0:T(8,128)(2,1)} custom-call(bf16[512,384]{1,0:T(8,128)(2,1)} %grad_ref.1, bf16[384,384]{1,0:T(8,128)(2,1)} %constant.8.clone.order_ref), custom_call_target="tpu_custom_call" | custom-call | flops 150994944 | bytes 3538944 | tf_op jit(solution)/shard_map/arrange/pallas_call | solution.py:92
  3.8 0.0 copy-start.2
  3.8 7.5 %all-to-all-start = ((bf16[8,512,384]{2,1,0:T(8,128)(2,1)}), bf16[8,512,384]{2,1,0:T(8,128)(2,1)S(1)}, u32[]{:S(2)}, u32[]{:S(2)}) async-start(bf16[8,512,384]{2,1,0:T(8,128)(2,1)} %arrange.1), calls=%async_computation | async-start | bytes 6291456 | tf_op jit(solution)/shard_map/all_to_all | solution.py:115
  11.3 0.0 copy-done.2
  11.3 47.7 %all-gather = bf16[192,384]{1,0:T(8,128)(2,1)S(1)} all-gather(bf16[24,384]{1,0:T(8,128)(2,1)S(1)} %copy-done.2), channel_id=2, replica_groups={{0,64,128,192,256,320,384,448},{8,72,136,200,264,328,392,456},{16,80,14..., dimensions={0}, use_global_device_ids=true | all-gather | bytes 165888 | tf_op jit(solution)/shard_map/all_gather | solution.py:42
  59.0 1.9 %collective-permute-start = (bf16[8,24,384]{2,1,0:T(8,128)(2,1)S(1)}, bf16[8,24,384]{2,1,0:T(8,128)(2,1)S(1)}, u32[]{:S(2)}, u32[]{:S(2)}) collective-permute-start(bf16[8,24,384]{2,1,0:T(8,128)(2,1)S(1)} %bitcast.13), channel_id=1, source_target_pairs={{0,512},{8,520},{16,528},{24,536},{32,544},{40,552},{48,560},{56,5... | collective-permute-start | bytes 442376 | tf_op jit(solution)/shard_map/ppermute | solution.py:53
  60.9 4.0 %collective-permute-done = bf16[8,24,384]{2,1,0:T(8,128)(2,1)S(1)} collective-permute-done((bf16[8,24,384]{2,1,0:T(8,128)(2,1)S(1)}, bf16[8,24,384]{2,1,0:T(8,128)(2,1)S(1)}, u32[]{:S(2)}, u32[]{:S(2)}) %collective-permute-start) | collective-permute-done | bytes 147488 | tf_op jit(solution)/shard_map/ppermute | solution.py:53
  64.9 0.0 copy-start.1
  64.9 0.0 all-to-all-done.blocks
  64.9 0.0 copy-start
  64.9 2.6 %collective-permute-start.3 = (bf16[2,8,24,384]{3,2,1,0:T(8,128)(2,1)S(1)}, bf16[2,8,24,384]{3,2,1,0:T(8,128)(2,1)}, u32[]{:S(2)}, u32[]{:S(2)}) collective-permute-start(bf16[2,8,24,384]{3,2,1,0:T(8,128)(2,1)S(1)} %pad_maximum_fusion), channel_id=1, source_target_pairs={{32,0},{488,8},{48,16},{504,24},{64,32},{8,40},{80,48},{24,56},{96... | collective-permute-start | bytes 884744 | tf_op jit(solution)/shard_map/ppermute | solution.py:49
  67.5 2.6 %collective-permute-start.2 = (bf16[2,8,24,384]{3,2,1,0:T(8,128)(2,1)S(1)}, bf16[2,8,24,384]{3,2,1,0:T(8,128)(2,1)}, u32[]{:S(2)}, u32[]{:S(2)}) collective-permute-start(bf16[2,8,24,384]{3,2,1,0:T(8,128)(2,1)S(1)} %pad_maximum_fusion), channel_id=1, source_target_pairs={{16,0},{504,8},{32,16},{8,24},{48,32},{24,40},{64,48},{40,56},{80,... | collective-permute-start | bytes 884744 | tf_op jit(solution)/shard_map/ppermute | solution.py:49
  70.1 3.9 %collective-permute-start.1 = (bf16[2,8,24,384]{3,2,1,0:T(8,128)(2,1)S(1)}, bf16[2,8,24,384]{3,2,1,0:T(8,128)(2,1)}, u32[]{:S(2)}, u32[]{:S(2)}) collective-permute-start(bf16[2,8,24,384]{3,2,1,0:T(8,128)(2,1)S(1)} %pad_maximum_fusion), channel_id=1, source_target_pairs={{496,0},{24,8},{0,16},{40,24},{16,32},{56,40},{32,48},{72,56},{48,... | collective-permute-start | bytes 884744 | tf_op jit(solution)/shard_map/ppermute | solution.py:49
  74.0 8.9 %collective-permute-start.4 = (bf16[2,8,24,384]{3,2,1,0:T(8,128)(2,1)S(1)}, bf16[2,8,24,384]{3,2,1,0:T(8,128)(2,1)}, u32[]{:S(2)}, u32[]{:S(2)}) collective-permute-start(bf16[2,8,24,384]{3,2,1,0:T(8,128)(2,1)S(1)} %pad_maximum_fusion), channel_id=1, source_target_pairs={{0,8},{8,0},{16,24},{24,16},{32,40},{40,32},{48,56},{56,48},{64,72... | collective-permute-start | bytes 884744 | tf_op jit(solution)/shard_map/ppermute | solution.py:59
  82.9 0.0 collective-permute-done.3
  82.9 4.6 %collective-permute-start.7 = (bf16[2,8,24,384]{3,2,1,0:T(8,128)(2,1)}, bf16[2,8,24,384]{3,2,1,0:T(8,128)(2,1)}, u32[]{:S(2)}, u32[]{:S(2)}) collective-permute-start(bf16[2,8,24,384]{3,2,1,0:T(8,128)(2,1)} %collective-permute-done.3), channel_id=1, source_target_pairs={{0,8},{8,0},{16,24},{24,16},{32,40},{40,32},{48,56},{56,48},{64,72... | collective-permute-start | bytes 884744 | tf_op jit(solution)/shard_map/ppermute | solution.py:59
  87.5 0.0 collective-permute-done.2
  87.5 2.2 %collective-permute-start.6 = (bf16[2,8,24,384]{3,2,1,0:T(8,128)(2,1)}, bf16[2,8,24,384]{3,2,1,0:T(8,128)(2,1)}, u32[]{:S(2)}, u32[]{:S(2)}) collective-permute-start(bf16[2,8,24,384]{3,2,1,0:T(8,128)(2,1)} %collective-permute-done.2), channel_id=1, source_target_pairs={{0,8},{8,0},{16,24},{24,16},{32,40},{40,32},{48,56},{56,48},{64,72... | collective-permute-start | bytes 884744 | tf_op jit(solution)/shard_map/ppermute | solution.py:59
  89.8 0.0 collective-permute-done.1
  89.8 2.1 %collective-permute-start.5 = (bf16[2,8,24,384]{3,2,1,0:T(8,128)(2,1)}, bf16[2,8,24,384]{3,2,1,0:T(8,128)(2,1)}, u32[]{:S(2)}, u32[]{:S(2)}) collective-permute-start(bf16[2,8,24,384]{3,2,1,0:T(8,128)(2,1)} %collective-permute-done.1), channel_id=1, source_target_pairs={{0,8},{8,0},{16,24},{24,16},{32,40},{40,32},{48,56},{56,48},{64,72... | collective-permute-start | bytes 884744 | tf_op jit(solution)/shard_map/ppermute | solution.py:59
  91.9 0.0 collective-permute-done.4
  91.9 0.0 collective-permute-done.7
  91.9 0.0 collective-permute-done.6
  91.9 1.7 %collective-permute-done.5 = bf16[2,8,24,384]{3,2,1,0:T(8,128)(2,1)} collective-permute-done((bf16[2,8,24,384]{3,2,1,0:T(8,128)(2,1)}, bf16[2,8,24,384]{3,2,1,0:T(8,128)(2,1)}, u32[]{:S(2)}, u32[]{:S(2)}) %collective-permute-start.5) | collective-permute-done | bytes 294944 | tf_op jit(solution)/shard_map/ppermute | solution.py:59
  93.6 0.0 copy-done.1
  93.6 0.0 copy-done
  93.6 8.2 %tail.1 = (bf16[512,384]{1,0:T(8,128)(2,1)}, bf16[512,384]{1,0:T(8,128)(2,1)}, bf16[512,384]{1,0:T(8,128)(2,1)}) custom-call(s32[1]{0:T(128)} %bitcast.here_ref, bf16[512,384]{1,0:T(8,128)(2,1)} %queries.1, bf16[512,384]{1,0:T(8,128)(2,1)} %keys.1, bf16[512,384]{1,0:T(8,128)(2,1)} %values.1, bf16[8,512,384]{2,1,0:T(8,128)(2,1)} %copy-done, ...), custom_call_target="tpu_custom_call" | custom-call | flops 1610612736 | bytes 8257536 | tf_op jit(solution)/shard_map/tail/pallas_call | solution.py:221
  (1 shorter events, 0.0 us)
Async XLA Ops:
  3.8 7.5 %copy-start.2 = (bf16[24,384]{1,0:T(8,128)(2,1)S(1)}, bf16[24,384]{1,0:T(8,128)(2,1)}, u32[]{:S(2)}) copy-start(bf16[24,384]{1,0:T(8,128)(2,1)} %param.10) | copy-start | bytes 55300
  3.8 61.1 %all-to-all-start = ((bf16[8,512,384]{2,1,0:T(8,128)(2,1)}), bf16[8,512,384]{2,1,0:T(8,128)(2,1)S(1)}, u32[]{:S(2)}, u32[]{:S(2)}) async-start(bf16[8,512,384]{2,1,0:T(8,128)(2,1)} %arrange.1), calls=%async_computation | async-start | bytes 6291456 | tf_op jit(solution)/shard_map/all_to_all | solution.py:115
  59.0 5.9 %collective-permute-start = (bf16[8,24,384]{2,1,0:T(8,128)(2,1)S(1)}, bf16[8,24,384]{2,1,0:T(8,128)(2,1)S(1)}, u32[]{:S(2)}, u32[]{:S(2)}) collective-permute-start(bf16[8,24,384]{2,1,0:T(8,128)(2,1)S(1)} %bitcast.13), channel_id=1, source_target_pairs={{0,512},{8,520},{16,528},{24,536},{32,544},{40,552},{48,560},{56,5... | collective-permute-start | bytes 442376 | tf_op jit(solution)/shard_map/ppermute | solution.py:53
  64.9 28.7 %copy-start.1 = (bf16[2,8,24,384]{3,2,1,0:T(8,128)(2,1)}, bf16[2,8,24,384]{3,2,1,0:T(8,128)(2,1)S(1)}, u32[]{:S(2)}) copy-start(bf16[2,8,24,384]{3,2,1,0:T(8,128)(2,1)S(1)} %pad_maximum_fusion) | copy-start | bytes 884740
  64.9 28.7 %copy-start = (bf16[8,512,384]{2,1,0:T(8,128)(2,1)}, bf16[8,512,384]{2,1,0:T(8,128)(2,1)S(1)}, u32[]{:S(2)}) copy-start(bf16[8,512,384]{2,1,0:T(8,128)(2,1)S(1)} %all-to-all-done.blocks) | copy-start | bytes 9437188
  64.9 18.0 %collective-permute-start.3 = (bf16[2,8,24,384]{3,2,1,0:T(8,128)(2,1)S(1)}, bf16[2,8,24,384]{3,2,1,0:T(8,128)(2,1)}, u32[]{:S(2)}, u32[]{:S(2)}) collective-permute-start(bf16[2,8,24,384]{3,2,1,0:T(8,128)(2,1)S(1)} %pad_maximum_fusion), channel_id=1, source_target_pairs={{32,0},{488,8},{48,16},{504,24},{64,32},{8,40},{80,48},{24,56},{96... | collective-permute-start | bytes 884744 | tf_op jit(solution)/shard_map/ppermute | solution.py:49
  67.5 20.0 %collective-permute-start.2 = (bf16[2,8,24,384]{3,2,1,0:T(8,128)(2,1)S(1)}, bf16[2,8,24,384]{3,2,1,0:T(8,128)(2,1)}, u32[]{:S(2)}, u32[]{:S(2)}) collective-permute-start(bf16[2,8,24,384]{3,2,1,0:T(8,128)(2,1)S(1)} %pad_maximum_fusion), channel_id=1, source_target_pairs={{16,0},{504,8},{32,16},{8,24},{48,32},{24,40},{64,48},{40,56},{80,... | collective-permute-start | bytes 884744 | tf_op jit(solution)/shard_map/ppermute | solution.py:49
  70.1 19.7 %collective-permute-start.1 = (bf16[2,8,24,384]{3,2,1,0:T(8,128)(2,1)S(1)}, bf16[2,8,24,384]{3,2,1,0:T(8,128)(2,1)}, u32[]{:S(2)}, u32[]{:S(2)}) collective-permute-start(bf16[2,8,24,384]{3,2,1,0:T(8,128)(2,1)S(1)} %pad_maximum_fusion), channel_id=1, source_target_pairs={{496,0},{24,8},{0,16},{40,24},{16,32},{56,40},{32,48},{72,56},{48,... | collective-permute-start | bytes 884744 | tf_op jit(solution)/shard_map/ppermute | solution.py:49
  74.0 17.8 %collective-permute-start.4 = (bf16[2,8,24,384]{3,2,1,0:T(8,128)(2,1)S(1)}, bf16[2,8,24,384]{3,2,1,0:T(8,128)(2,1)}, u32[]{:S(2)}, u32[]{:S(2)}) collective-permute-start(bf16[2,8,24,384]{3,2,1,0:T(8,128)(2,1)S(1)} %pad_maximum_fusion), channel_id=1, source_target_pairs={{0,8},{8,0},{16,24},{24,16},{32,40},{40,32},{48,56},{56,48},{64,72... | collective-permute-start | bytes 884744 | tf_op jit(solution)/shard_map/ppermute | solution.py:59
  82.9 9.0 %collective-permute-start.7 = (bf16[2,8,24,384]{3,2,1,0:T(8,128)(2,1)}, bf16[2,8,24,384]{3,2,1,0:T(8,128)(2,1)}, u32[]{:S(2)}, u32[]{:S(2)}) collective-permute-start(bf16[2,8,24,384]{3,2,1,0:T(8,128)(2,1)} %collective-permute-done.3), channel_id=1, source_target_pairs={{0,8},{8,0},{16,24},{24,16},{32,40},{40,32},{48,56},{56,48},{64,72... | collective-permute-start | bytes 884744 | tf_op jit(solution)/shard_map/ppermute | solution.py:59
  87.5 4.4 %collective-permute-start.6 = (bf16[2,8,24,384]{3,2,1,0:T(8,128)(2,1)}, bf16[2,8,24,384]{3,2,1,0:T(8,128)(2,1)}, u32[]{:S(2)}, u32[]{:S(2)}) collective-permute-start(bf16[2,8,24,384]{3,2,1,0:T(8,128)(2,1)} %collective-permute-done.2), channel_id=1, source_target_pairs={{0,8},{8,0},{16,24},{24,16},{32,40},{40,32},{48,56},{56,48},{64,72... | collective-permute-start | bytes 884744 | tf_op jit(solution)/shard_map/ppermute | solution.py:59
  89.8 3.8 %collective-permute-start.5 = (bf16[2,8,24,384]{3,2,1,0:T(8,128)(2,1)}, bf16[2,8,24,384]{3,2,1,0:T(8,128)(2,1)}, u32[]{:S(2)}, u32[]{:S(2)}) collective-permute-start(bf16[2,8,24,384]{3,2,1,0:T(8,128)(2,1)} %collective-permute-done.1), channel_id=1, source_target_pairs={{0,8},{8,0},{16,24},{24,16},{32,40},{40,32},{48,56},{56,48},{64,72... | collective-permute-start | bytes 884744 | tf_op jit(solution)/shard_map/ppermute | solution.py:59

commit v6 on v4

--- a/solution.py
+++ b/solution.py
@@ -165,14 +165,14 @@
         copy.wait()
     for image in range(images):
         rows = pl.ds(image * PATCHES, PATCHES)
-        total = None
-        for j in range(count):
-            if image == 0:
-                copies[18 + j].wait()
-            product = jnp.dot(
-                blocks_ref[j, rows, :], weight_ref[j], preferred_element_type=jnp.float32
-            )
-            total = product if total is None else total + product
+        if image == 0:
+            for copy in copies[18:-1]:
+                copy.wait()
+        total = jnp.dot(
+            jnp.concatenate([blocks_ref[j, rows, :] for j in range(count)], axis=1),
+            weight_ref[...].reshape(count * weight_ref.shape[1], weight_ref.shape[2]),
+            preferred_element_type=jnp.float32,
+        )
         if image == 0:
             copies[-1].wait()
         grad_image = total.astype(jnp.bfloat16)

time: 102 us -> 102 us (level)
  no operation moved by 1% of the time
where the time goes in v6:
time: 102 us
  blocking collectives  47.7 us (47%)
  starting transfers between devices  36.3 us (36%)
  Pallas kernels  11.1 us (11%)
  waiting for transfers between devices  5.65 us (6%)
    all_gather x1, blocking collectives, far_rows(): return lax.all_gather(weight, 'dp', axis_index_groups=groups)  47.7 us
    ppermute x4, starting transfers between devices, core_swap(): lax.ppermute(array, 'dp', [(dp_index(x, z, c), dp_index(x, z, 1 - c)) for...  17.8 us
    ppermute x3, starting transfers between devices, z_shift(): return lax.ppermute(array, 'dp', pairs)  9.1 us
    pallas_call x1, Pallas kernels, body(): pl.pallas_call(functools.partial(tail_kernel, images, heads), out_shape=(...  7.93 us
    all_to_all x1, starting transfers between devices, gather_both(): lax.all_to_all(arranged_copies(grad, Y * XHI), 'mp', 0, 0, tiled=True)  7.49 us
    ppermute x1, waiting for transfers between devices, x_swap(): lax.ppermute(array, 'dp', [(dp_index(x, z, c), dp_index(1 - x, z, c)) for...  3.96 us
    pallas_call x1, Pallas kernels, arranged_copies(): pl.pallas_call(arrange_kernel, out_shape=jax.ShapeDtypeStruct((count, row...  3.17 us
  transfers between devices with their start and end apart: 9, of which 2 were waited for; matrix products, arithmetic and copies ran while one was open for 0% of the time, Pallas kernels for 0%

profile of v6, /device:TPU:1, one launch (start us, length us, event | category | flops | bytes accessed | tf_op | source)
XLA Modules:
  0.0 101.6 jit_solution(6158520727092737940)
XLA Ops:
  0.6 3.2 %arrange.1 = bf16[8,512,384]{2,1,0:T(8,128)(2,1)} custom-call(bf16[512,384]{1,0:T(8,128)(2,1)} %grad_ref.1, bf16[384,384]{1,0:T(8,128)(2,1)} %constant.8.clone.order_ref), custom_call_target="tpu_custom_call" | custom-call | flops 150994944 | bytes 3538944 | tf_op jit(solution)/shard_map/arrange/pallas_call | solution.py:90
  3.8 0.0 copy-start.2
  3.8 7.5 %all-to-all-start = ((bf16[8,512,384]{2,1,0:T(8,128)(2,1)}), bf16[8,512,384]{2,1,0:T(8,128)(2,1)S(1)}, u32[]{:S(2)}, u32[]{:S(2)}) async-start(bf16[8,512,384]{2,1,0:T(8,128)(2,1)} %arrange.1), calls=%async_computation | async-start | bytes 6291456 | tf_op jit(solution)/shard_map/all_to_all | solution.py:113
  11.3 0.0 copy-done.2
  11.3 47.7 %all-gather = bf16[192,384]{1,0:T(8,128)(2,1)S(1)} all-gather(bf16[24,384]{1,0:T(8,128)(2,1)S(1)} %copy-done.2), channel_id=2, replica_groups={{0,64,128,192,256,320,384,448},{8,72,136,200,264,328,392,456},{16,80,14..., dimensions={0}, use_global_device_ids=true | all-gather | bytes 165888 | tf_op jit(solution)/shard_map/all_gather | solution.py:42
  59.0 1.9 %collective-permute-start = (bf16[8,24,384]{2,1,0:T(8,128)(2,1)S(1)}, bf16[8,24,384]{2,1,0:T(8,128)(2,1)S(1)}, u32[]{:S(2)}, u32[]{:S(2)}) collective-permute-start(bf16[8,24,384]{2,1,0:T(8,128)(2,1)S(1)} %bitcast.13), channel_id=1, source_target_pairs={{0,512},{8,520},{16,528},{24,536},{32,544},{40,552},{48,560},{56,5... | collective-permute-start | bytes 442376 | tf_op jit(solution)/shard_map/ppermute | solution.py:53
  60.9 4.0 %collective-permute-done = bf16[8,24,384]{2,1,0:T(8,128)(2,1)S(1)} collective-permute-done((bf16[8,24,384]{2,1,0:T(8,128)(2,1)S(1)}, bf16[8,24,384]{2,1,0:T(8,128)(2,1)S(1)}, u32[]{:S(2)}, u32[]{:S(2)}) %collective-permute-start) | collective-permute-done | bytes 147488 | tf_op jit(solution)/shard_map/ppermute | solution.py:53
  64.9 0.0 copy-start.1
  64.9 0.0 all-to-all-done.blocks
  64.9 0.0 copy-start
  65.0 2.6 %collective-permute-start.3 = (bf16[2,8,24,384]{3,2,1,0:T(8,128)(2,1)S(1)}, bf16[2,8,24,384]{3,2,1,0:T(8,128)(2,1)}, u32[]{:S(2)}, u32[]{:S(2)}) collective-permute-start(bf16[2,8,24,384]{3,2,1,0:T(8,128)(2,1)S(1)} %pad_maximum_fusion), channel_id=1, source_target_pairs={{32,0},{488,8},{48,16},{504,24},{64,32},{8,40},{80,48},{24,56},{96... | collective-permute-start | bytes 884744 | tf_op jit(solution)/shard_map/ppermute | solution.py:49
  67.6 2.6 %collective-permute-start.2 = (bf16[2,8,24,384]{3,2,1,0:T(8,128)(2,1)S(1)}, bf16[2,8,24,384]{3,2,1,0:T(8,128)(2,1)}, u32[]{:S(2)}, u32[]{:S(2)}) collective-permute-start(bf16[2,8,24,384]{3,2,1,0:T(8,128)(2,1)S(1)} %pad_maximum_fusion), channel_id=1, source_target_pairs={{16,0},{504,8},{32,16},{8,24},{48,32},{24,40},{64,48},{40,56},{80,... | collective-permute-start | bytes 884744 | tf_op jit(solution)/shard_map/ppermute | solution.py:49
  70.1 3.9 %collective-permute-start.1 = (bf16[2,8,24,384]{3,2,1,0:T(8,128)(2,1)S(1)}, bf16[2,8,24,384]{3,2,1,0:T(8,128)(2,1)}, u32[]{:S(2)}, u32[]{:S(2)}) collective-permute-start(bf16[2,8,24,384]{3,2,1,0:T(8,128)(2,1)S(1)} %pad_maximum_fusion), channel_id=1, source_target_pairs={{496,0},{24,8},{0,16},{40,24},{16,32},{56,40},{32,48},{72,56},{48,... | collective-permute-start | bytes 884744 | tf_op jit(solution)/shard_map/ppermute | solution.py:49
  74.1 8.9 %collective-permute-start.4 = (bf16[2,8,24,384]{3,2,1,0:T(8,128)(2,1)S(1)}, bf16[2,8,24,384]{3,2,1,0:T(8,128)(2,1)}, u32[]{:S(2)}, u32[]{:S(2)}) collective-permute-start(bf16[2,8,24,384]{3,2,1,0:T(8,128)(2,1)S(1)} %pad_maximum_fusion), channel_id=1, source_target_pairs={{0,8},{8,0},{16,24},{24,16},{32,40},{40,32},{48,56},{56,48},{64,72... | collective-permute-start | bytes 884744 | tf_op jit(solution)/shard_map/ppermute | solution.py:59
  82.9 0.0 collective-permute-done.3
  83.0 4.6 %collective-permute-start.7 = (bf16[2,8,24,384]{3,2,1,0:T(8,128)(2,1)}, bf16[2,8,24,384]{3,2,1,0:T(8,128)(2,1)}, u32[]{:S(2)}, u32[]{:S(2)}) collective-permute-start(bf16[2,8,24,384]{3,2,1,0:T(8,128)(2,1)} %collective-permute-done.3), channel_id=1, source_target_pairs={{0,8},{8,0},{16,24},{24,16},{32,40},{40,32},{48,56},{56,48},{64,72... | collective-permute-start | bytes 884744 | tf_op jit(solution)/shard_map/ppermute | solution.py:59
  87.5 0.0 collective-permute-done.2
  87.6 2.2 %collective-permute-start.6 = (bf16[2,8,24,384]{3,2,1,0:T(8,128)(2,1)}, bf16[2,8,24,384]{3,2,1,0:T(8,128)(2,1)}, u32[]{:S(2)}, u32[]{:S(2)}) collective-permute-start(bf16[2,8,24,384]{3,2,1,0:T(8,128)(2,1)} %collective-permute-done.2), channel_id=1, source_target_pairs={{0,8},{8,0},{16,24},{24,16},{32,40},{40,32},{48,56},{56,48},{64,72... | collective-permute-start | bytes 884744 | tf_op jit(solution)/shard_map/ppermute | solution.py:59
  89.8 0.0 collective-permute-done.1
  89.8 2.1 %collective-permute-start.5 = (bf16[2,8,24,384]{3,2,1,0:T(8,128)(2,1)}, bf16[2,8,24,384]{3,2,1,0:T(8,128)(2,1)}, u32[]{:S(2)}, u32[]{:S(2)}) collective-permute-start(bf16[2,8,24,384]{3,2,1,0:T(8,128)(2,1)} %collective-permute-done.1), channel_id=1, source_target_pairs={{0,8},{8,0},{16,24},{24,16},{32,40},{40,32},{48,56},{56,48},{64,72... | collective-permute-start | bytes 884744 | tf_op jit(solution)/shard_map/ppermute | solution.py:59
  91.9 0.0 collective-permute-done.4
  91.9 0.0 collective-permute-done.7
  91.9 0.0 collective-permute-done.6
  91.9 1.7 %collective-permute-done.5 = bf16[2,8,24,384]{3,2,1,0:T(8,128)(2,1)} collective-permute-done((bf16[2,8,24,384]{3,2,1,0:T(8,128)(2,1)}, bf16[2,8,24,384]{3,2,1,0:T(8,128)(2,1)}, u32[]{:S(2)}, u32[]{:S(2)}) %collective-permute-start.5) | collective-permute-done | bytes 294944 | tf_op jit(solution)/shard_map/ppermute | solution.py:59
  93.6 0.0 copy-done.1
  93.6 0.0 copy-done
  93.6 7.9 %tail.1 = (bf16[512,384]{1,0:T(8,128)(2,1)}, bf16[512,384]{1,0:T(8,128)(2,1)}, bf16[512,384]{1,0:T(8,128)(2,1)}) custom-call(s32[1]{0:T(128)} %bitcast.here_ref, bf16[512,384]{1,0:T(8,128)(2,1)} %queries.1, bf16[512,384]{1,0:T(8,128)(2,1)} %keys.1, bf16[512,384]{1,0:T(8,128)(2,1)} %values.1, bf16[8,512,384]{2,1,0:T(8,128)(2,1)} %copy-done, ...), custom_call_target="tpu_custom_call" | custom-call | flops 1610612736 | bytes 8257536 | tf_op jit(solution)/shard_map/tail/pallas_call | solution.py:209
  (1 shorter events, 0.0 us)
Async XLA Ops:
  3.8 7.5 %copy-start.2 = (bf16[24,384]{1,0:T(8,128)(2,1)S(1)}, bf16[24,384]{1,0:T(8,128)(2,1)}, u32[]{:S(2)}) copy-start(bf16[24,384]{1,0:T(8,128)(2,1)} %param.10) | copy-start | bytes 55300
  3.8 61.1 %all-to-all-start = ((bf16[8,512,384]{2,1,0:T(8,128)(2,1)}), bf16[8,512,384]{2,1,0:T(8,128)(2,1)S(1)}, u32[]{:S(2)}, u32[]{:S(2)}) async-start(bf16[8,512,384]{2,1,0:T(8,128)(2,1)} %arrange.1), calls=%async_computation | async-start | bytes 6291456 | tf_op jit(solution)/shard_map/all_to_all | solution.py:113
  59.0 5.9 %collective-permute-start = (bf16[8,24,384]{2,1,0:T(8,128)(2,1)S(1)}, bf16[8,24,384]{2,1,0:T(8,128)(2,1)S(1)}, u32[]{:S(2)}, u32[]{:S(2)}) collective-permute-start(bf16[8,24,384]{2,1,0:T(8,128)(2,1)S(1)} %bitcast.13), channel_id=1, source_target_pairs={{0,512},{8,520},{16,528},{24,536},{32,544},{40,552},{48,560},{56,5... | collective-permute-start | bytes 442376 | tf_op jit(solution)/shard_map/ppermute | solution.py:53
  64.9 28.7 %copy-start.1 = (bf16[2,8,24,384]{3,2,1,0:T(8,128)(2,1)}, bf16[2,8,24,384]{3,2,1,0:T(8,128)(2,1)S(1)}, u32[]{:S(2)}) copy-start(bf16[2,8,24,384]{3,2,1,0:T(8,128)(2,1)S(1)} %pad_maximum_fusion) | copy-start | bytes 884740
  64.9 28.7 %copy-start = (bf16[8,512,384]{2,1,0:T(8,128)(2,1)}, bf16[8,512,384]{2,1,0:T(8,128)(2,1)S(1)}, u32[]{:S(2)}) copy-start(bf16[8,512,384]{2,1,0:T(8,128)(2,1)S(1)} %all-to-all-done.blocks) | copy-start | bytes 9437188
  65.0 18.0 %collective-permute-start.3 = (bf16[2,8,24,384]{3,2,1,0:T(8,128)(2,1)S(1)}, bf16[2,8,24,384]{3,2,1,0:T(8,128)(2,1)}, u32[]{:S(2)}, u32[]{:S(2)}) collective-permute-start(bf16[2,8,24,384]{3,2,1,0:T(8,128)(2,1)S(1)} %pad_maximum_fusion), channel_id=1, source_target_pairs={{32,0},{488,8},{48,16},{504,24},{64,32},{8,40},{80,48},{24,56},{96... | collective-permute-start | bytes 884744 | tf_op jit(solution)/shard_map/ppermute | solution.py:49
  67.6 20.0 %collective-permute-start.2 = (bf16[2,8,24,384]{3,2,1,0:T(8,128)(2,1)S(1)}, bf16[2,8,24,384]{3,2,1,0:T(8,128)(2,1)}, u32[]{:S(2)}, u32[]{:S(2)}) collective-permute-start(bf16[2,8,24,384]{3,2,1,0:T(8,128)(2,1)S(1)} %pad_maximum_fusion), channel_id=1, source_target_pairs={{16,0},{504,8},{32,16},{8,24},{48,32},{24,40},{64,48},{40,56},{80,... | collective-permute-start | bytes 884744 | tf_op jit(solution)/shard_map/ppermute | solution.py:49
  70.1 19.7 %collective-permute-start.1 = (bf16[2,8,24,384]{3,2,1,0:T(8,128)(2,1)S(1)}, bf16[2,8,24,384]{3,2,1,0:T(8,128)(2,1)}, u32[]{:S(2)}, u32[]{:S(2)}) collective-permute-start(bf16[2,8,24,384]{3,2,1,0:T(8,128)(2,1)S(1)} %pad_maximum_fusion), channel_id=1, source_target_pairs={{496,0},{24,8},{0,16},{40,24},{16,32},{56,40},{32,48},{72,56},{48,... | collective-permute-start | bytes 884744 | tf_op jit(solution)/shard_map/ppermute | solution.py:49
  74.1 17.8 %collective-permute-start.4 = (bf16[2,8,24,384]{3,2,1,0:T(8,128)(2,1)S(1)}, bf16[2,8,24,384]{3,2,1,0:T(8,128)(2,1)}, u32[]{:S(2)}, u32[]{:S(2)}) collective-permute-start(bf16[2,8,24,384]{3,2,1,0:T(8,128)(2,1)S(1)} %pad_maximum_fusion), channel_id=1, source_target_pairs={{0,8},{8,0},{16,24},{24,16},{32,40},{40,32},{48,56},{56,48},{64,72... | collective-permute-start | bytes 884744 | tf_op jit(solution)/shard_map/ppermute | solution.py:59
  83.0 9.0 %collective-permute-start.7 = (bf16[2,8,24,384]{3,2,1,0:T(8,128)(2,1)}, bf16[2,8,24,384]{3,2,1,0:T(8,128)(2,1)}, u32[]{:S(2)}, u32[]{:S(2)}) collective-permute-start(bf16[2,8,24,384]{3,2,1,0:T(8,128)(2,1)} %collective-permute-done.3), channel_id=1, source_target_pairs={{0,8},{8,0},{16,24},{24,16},{32,40},{40,32},{48,56},{56,48},{64,72... | collective-permute-start | bytes 884744 | tf_op jit(solution)/shard_map/ppermute | solution.py:59
  87.6 4.4 %collective-permute-start.6 = (bf16[2,8,24,384]{3,2,1,0:T(8,128)(2,1)}, bf16[2,8,24,384]{3,2,1,0:T(8,128)(2,1)}, u32[]{:S(2)}, u32[]{:S(2)}) collective-permute-start(bf16[2,8,24,384]{3,2,1,0:T(8,128)(2,1)} %collective-permute-done.2), channel_id=1, source_target_pairs={{0,8},{8,0},{16,24},{24,16},{32,40},{40,32},{48,56},{56,48},{64,72... | collective-permute-start | bytes 884744 | tf_op jit(solution)/shard_map/ppermute | solution.py:59
  89.8 3.8 %collective-permute-start.5 = (bf16[2,8,24,384]{3,2,1,0:T(8,128)(2,1)}, bf16[2,8,24,384]{3,2,1,0:T(8,128)(2,1)}, u32[]{:S(2)}, u32[]{:S(2)}) collective-permute-start(bf16[2,8,24,384]{3,2,1,0:T(8,128)(2,1)} %collective-permute-done.1), channel_id=1, source_target_pairs={{0,8},{8,0},{16,24},{24,16},{32,40},{40,32},{48,56},{56,48},{64,72... | collective-permute-start | bytes 884744 | tf_op jit(solution)/shard_map/ppermute | solution.py:59
